TPU v7x, 32 devices: a whole 2x2x4 slice. The times are simulated.
32 devices in a mesh: groups: 2 (over x), ctx: 16 (over z, y, core).
Axes of the slice: x: 2, y: 2, z: 4, core: 2. Of those that a mesh axis runs over, the one named last changes fastest.
Arguments:
- hidden: bfloat16 [4096, 4096], P(('groups', 'ctx')), parts along dimension 0, may hold values from -6 to 6
- frozen_query: bfloat16 [4096, 2048], P(('groups', 'ctx')), parts along dimension 0, may hold values from -18 to 18
- frozen_key: bfloat16 [4096, 512], P(('groups', 'ctx')), parts along dimension 0, may hold values from -18 to 18
- frozen_value: bfloat16 [4096, 512], P(('groups', 'ctx')), parts along dimension 0, may hold values from -6 to 6
- adapter_bank: bfloat16 [16, 64, 21504], P('ctx'), may hold values from -0.57 to 0.57
- request_shards: int32 [6], P('groups'), parts along dimension 0, may hold values from 1 to 9, 16 in all
- request_adapter: int32 [6], P('groups'), parts along dimension 0, may hold values from 0 to 15
- adapter_owner: int32 [16], replicated, may hold values from 0 to 15, each once
Outputs:
- attention: bfloat16 [4096, 2048], P(('groups', 'ctx')), parts along dimension 0
- adapter_output: bfloat16 [4096, 4096], P(('groups', 'ctx')), parts along dimension 0
There are 2 independent parts, one for each index of `groups`. A program takes and returns all parts, laid end to end along the dimension named above; an argument that names none is the same for every part. Nothing has to cross between parts.
Inputs may be any that keep to these rules, and one draw needn't show every extreme that they name: `request_shards`: request lengths sum to 16; the longest has exactly 9 shards. `adapter_owner`: a permutation: every bank entry holds exactly one adapter.
All inputs are finite; a program needn't handle non-finite values.
Results may differ from a plain program's by a relative error of at most 0.012.
Values may be sent and summed in bfloat16 or wider, within the bound.
No kernel may reach another device: no remote copies, remote signals or barrier semaphores. Data moves between devices by JAX's collectives and lax.ppermute only.
A program may use at most 64 MiB of HBM per device.

v0:
```python
import functools

import jax
import jax.numpy as jnp
from jax import lax
from jax.experimental import pallas as pl
from jax.experimental.pallas import tpu as pltpu
from jax.sharding import PartitionSpec as P

HEAD_SIZE = 128
QUERY_HEADS = 16
KEY_VALUE_HEADS = 4
GROUP_SPLIT = QUERY_HEADS // KEY_VALUE_HEADS

adapter_scale = 0.5
rope_theta = 500000.0
score_masked = -1e30

VMEM_LIMIT = 24 * 1024 * 1024

ROW_BLOCKS = 4
CHUNKS = 8


def rope_tables(positions):
    half_dim = HEAD_SIZE // 2
    frequency = rope_theta ** (-(jnp.arange(half_dim, dtype=jnp.float32) * 2.0) / HEAD_SIZE)
    angles = positions.astype(jnp.float32)[..., None] * frequency
    cosines = jnp.cos(angles)
    sines = jnp.sin(angles)
    return (jnp.concatenate([cosines, cosines], -1), jnp.concatenate([-sines, sines], -1))


class Parts:
    def __init__(self, model_width, query_width, key_width):
        d, q, k = model_width, query_width, key_width
        up = 3 * d
        self.kv = ((d, d // CHUNKS), (2 * d, d // CHUNKS), (up + q, 2 * k // CHUNKS))
        self.q = ((0, d // CHUNKS), (up, q // CHUNKS))
        self.o = ((up + q + 2 * k, q // CHUNKS), (up + 2 * q + 2 * k, d // CHUNKS))
        self.all = self.kv + self.q + self.o
        self.widths = tuple(sum(w for _, w in part) for part in (self.kv, self.q, self.o))


def vmem(count=1):
    return [pl.BlockSpec(memory_space=pltpu.VMEM)] * count


def smem(count=1):
    return [pl.BlockSpec(memory_space=pltpu.SMEM)] * count


PARAMS = pltpu.CompilerParams(vmem_limit_bytes=VMEM_LIMIT)


OWN_INDEX, OWN_HALF, COUNT, ENTRY = 0, 1, 2, 8


def layout(lengths_ref, which, shards):
    starts, start, length = [jnp.int32(0)], jnp.int32(0), lengths_ref[which, 0]
    for r in range(1, lengths_ref.shape[1]):
        starts.append(starts[-1] + lengths_ref[which, r - 1])
        longer = lengths_ref[which, r] > length
        start = jnp.where(longer, starts[-1], start)
        length = jnp.where(longer, lengths_ref[which, r], length)
    return starts, start + lax.div(length, 2)


def plan_kernel(shards, reach, me_ref, lengths_ref, adapters_ref, owner_ref, out_ref):
    own_index, own_half = me_ref[0], me_ref[1]
    starts, offset = layout(lengths_ref, 0, shards)
    own_packed = lax.rem(own_index + offset, shards)
    first = jnp.int32(0)
    for start in starts[1:]:
        first = jnp.where(start <= own_packed, start, first)
    out_ref[OWN_INDEX] = own_index
    out_ref[OWN_HALF] = own_half
    out_ref[COUNT] = jnp.minimum(own_packed - first, reach) + 1
    for which in range(lengths_ref.shape[0]):
        starts, offset = layout(lengths_ref, which, shards)
        entries = [owner_ref[adapters_ref[which, r]] for r in range(len(starts))]
        at = ENTRY + shards * (own_half if which == 0 else 1 - own_half)
        for shard in range(shards):
            packed = lax.rem(shard + offset, shards)
            entry = entries[0]
            for start, later in zip(starts[1:], entries[1:]):
                entry = jnp.where(start <= packed, later, entry)
            out_ref[at + shard] = entry


def make_plan(shards, reach, me, lengths, adapters, owner):
    return pl.pallas_call(
        functools.partial(plan_kernel, shards, reach),
        out_shape=jax.ShapeDtypeStruct((ENTRY + lengths.shape[0] * shards,), jnp.int32),
        in_specs=smem(4),
        out_specs=smem()[0],
        name="plan",
    )(me, lengths, adapters, owner)


def pack_kernel(parts, halves, x_ref, bank_ref, out):
    own_half = x_ref[1]
    for block in range(out.shape[0]):
        piece = block % (ROW_BLOCKS * CHUNKS // halves)
        rows = pl.ds((piece % ROW_BLOCKS) * 16, 16)
        chunk = (piece // ROW_BLOCKS) * halves + own_half
        at = 0
        for first, width in parts.all:
            start = pl.multiple_of(first + chunk * width, 128)
            out[block, :, at : at + width] = bank_ref[0, rows, pl.ds(start, width)]
            at += width


def pack(parts, halves, shards, me, bank):
    width = sum(parts.widths)
    return pl.pallas_call(
        functools.partial(pack_kernel, parts, halves),
        out_shape=jax.ShapeDtypeStruct((shards, 16, width), bank.dtype),
        in_specs=smem() + vmem(),
        out_specs=vmem()[0],
        compiler_params=PARAMS,
        name="pack",
    )(me, bank)


ROUTE_STEPS = 4


def route_kernel(plan_ref, spread_ref, *outs):
    number = outs[0].shape[0]
    for i in range(number):
        entry = plan_ref[ENTRY + pl.program_id(0) * number + i]
        at = 0
        for out in outs:
            out[i] = spread_ref[entry, :, at : at + out.shape[2]]
            at += out.shape[2]


def route(plan, spread, first_width):
    dests = plan.shape[0] - ENTRY
    widths = (first_width, spread.shape[2] - first_width)
    return pl.pallas_call(
        route_kernel,
        out_shape=[jax.ShapeDtypeStruct((dests, 16, w), spread.dtype) for w in widths],
        grid=(ROUTE_STEPS,),
        in_specs=smem() + vmem(),
        out_specs=[
            pl.BlockSpec((dests // ROUTE_STEPS, 16, w), lambda i: (i, 0, 0)) for w in widths
        ],
        compiler_params=PARAMS,
        name="route",
    )(plan, spread)


def factor(piece_ref, chunk, at, width):
    halves = piece_ref.shape[0]
    place = chunk // halves * ROW_BLOCKS
    rows = piece_ref[chunk % halves, place : place + ROW_BLOCKS, :, at : at + width]
    return rows.reshape(ROW_BLOCKS * 16, width)


def columns(chunk, width):
    return slice(chunk * width, (chunk + 1) * width)


def dot_nt(a, b):
    return lax.dot_general(a, b, (((1,), (1,)), ((), ())), preferred_element_type=jnp.float32)


def turn(x, cosines, sines):
    return x * cosines + pltpu.roll(x, HEAD_SIZE // 2, 1) * sines


def kv_kernel(plan_ref, hidden_ref, key_ref, value_ref, cos_ref, sin_ref, piece_ref, out_ref):
    d = hidden_ref.shape[1] // CHUNKS
    rank = ROW_BLOCKS * 16
    low = jnp.zeros((hidden_ref.shape[0], 2 * rank), jnp.float32)
    for chunk in range(CHUNKS):
        down = jnp.concatenate(
            [factor(piece_ref, chunk, 0, d), factor(piece_ref, chunk, d, d)], axis=0
        )
        low += dot_nt(hidden_ref[:, columns(chunk, d)], down)
    low = low.astype(jnp.bfloat16)
    width = 2 * key_ref.shape[1] // CHUNKS
    own = plan_ref[COUNT] - 1
    cosines, sines = cos_ref[own], sin_ref[own]
    for chunk in range(CHUNKS):
        is_key = chunk < CHUNKS // 2
        up = factor(piece_ref, chunk, 2 * d, width)
        part = low[:, :rank] if is_key else low[:, rank:]
        update = jnp.dot(part, up, preferred_element_type=jnp.float32)
        frozen = (key_ref if is_key else value_ref)[:, columns(chunk % (CHUNKS // 2), width)]
        result = frozen.astype(jnp.float32) + adapter_scale * update
        if is_key:
            result = turn(result, cosines, sines)
        out_ref[:, columns(chunk, width)] = result.astype(jnp.bfloat16)


def make_keys_values(plan, hidden, key, value, tables, pieces):
    return pl.pallas_call(
        kv_kernel,
        out_shape=jax.ShapeDtypeStruct((key.shape[0], 2 * key.shape[1]), jnp.bfloat16),
        in_specs=smem() + vmem(6),
        out_specs=vmem()[0],
        compiler_params=PARAMS,
        cost_estimate=pl.CostEstimate(
            flops=150_000_000, bytes_accessed=3 << 20, transcendentals=0
        ),
        name="keys_values",
    )(plan, hidden, key, value, *tables, pieces)


def query_kernel(at, plan_ref, hidden_ref, query_ref, cos_ref, sin_ref, piece_ref, out_ref):
    tokens = query_ref.shape[0]
    d = hidden_ref.shape[1] // CHUNKS
    width = query_ref.shape[1] // CHUNKS
    low = jnp.zeros((tokens, ROW_BLOCKS * 16), jnp.float32)
    for chunk in range(CHUNKS):
        low += dot_nt(hidden_ref[:, columns(chunk, d)], factor(piece_ref, chunk, at, d))
    low = low.astype(jnp.bfloat16)
    own = plan_ref[COUNT] - 1
    cosines, sines = cos_ref[own], sin_ref[own]
    for chunk in range(CHUNKS):
        up = factor(piece_ref, chunk, at + d, width)
        update = jnp.dot(low, up, preferred_element_type=jnp.float32)
        result = query_ref[:, columns(chunk, width)].astype(jnp.float32) + adapter_scale * update
        for part in range(width // HEAD_SIZE):
            head = chunk * (width // HEAD_SIZE) + part
            turned = turn(result[:, columns(part, HEAD_SIZE)], cosines, sines)
            out_ref[head // GROUP_SPLIT, pl.ds((head % GROUP_SPLIT) * tokens, tokens)] = (
                turned.astype(jnp.bfloat16)
            )


def make_queries(plan, hidden, query, tables, pieces, at):
    tokens = hidden.shape[0]
    return pl.pallas_call(
        functools.partial(query_kernel, at),
        out_shape=jax.ShapeDtypeStruct(
            (KEY_VALUE_HEADS, GROUP_SPLIT * tokens, HEAD_SIZE), jnp.bfloat16
        ),
        in_specs=smem() + vmem(5),
        out_specs=vmem()[0],
        compiler_params=PARAMS,
        cost_estimate=pl.CostEstimate(
            flops=100_000_000, bytes_accessed=3 << 20, transcendentals=0
        ),
        name="queries",
    )(plan, hidden, query, *tables, pieces)


REGION = 5


def attend_kernel(steps, plan_ref, queries, *refs):
    blocks, (out_ref, copy_ref, high, acc) = refs[:-4], refs[-4:]
    count = plan_ref[COUNT]
    odd = lax.rem(plan_ref[OWN_INDEX], 2)
    aside = 2 * odd - 1
    steps = [s if even else s + aside for s, even in steps]
    tokens = out_ref.shape[0]
    rows = GROUP_SPLIT * tokens
    bf16 = jnp.bfloat16
    base2 = 1.4426950408889634 / (HEAD_SIZE**0.5)
    ones = jnp.ones((tokens, HEAD_SIZE), bf16)

    def region(first, number):
        shards = blocks[first : first + number]
        for g in range(KEY_VALUE_HEADS):
            keys = [b[:, columns(g, HEAD_SIZE)] for b in shards]
            values = [
                jnp.concatenate([b[:, columns(KEY_VALUE_HEADS + g, HEAD_SIZE)], ones], axis=1)
                for b in shards
            ]
            score = dot_nt(queries[g], jnp.concatenate(keys, axis=0))
            tiles = [score[:, columns(i, tokens)] for i in range(number)]
            if first == 0:
                row = lax.broadcasted_iota(jnp.int32, (rows, tokens), 0) % tokens
                column = lax.broadcasted_iota(jnp.int32, (rows, tokens), 1)
                tiles = [jnp.where(column <= row, tiles[0], score_masked)]
            else:
                tiles = [
                    jnp.where((step > 0) & (step < count), tile, score_masked)
                    for step, tile in zip(steps[first : first + number], tiles)
                ]
            top = functools.reduce(jnp.maximum, tiles)
            top = jnp.max(top, axis=1, keepdims=True) * base2
            top = jnp.broadcast_to(top, (rows, HEAD_SIZE))
            if first:
                old = high[g]
                top = jnp.maximum(old, top)
            weight = [jnp.exp2(t * base2 - top).astype(bf16) for t in tiles]
            blend = jnp.dot(
                jnp.concatenate(weight, axis=1),
                jnp.concatenate(values, axis=0),
                preferred_element_type=jnp.float32,
            )
            if first:
                shrink = jnp.exp2(old - top)
                blend += acc[g] * jnp.concatenate([shrink, shrink], axis=1)
            high[g] = top
            acc[g] = blend

    region(0, 1)
    for first in range(1, len(blocks), REGION):
        number = min(REGION, len(blocks) - first)
        nearest = functools.reduce(jnp.minimum, steps[first : first + number])
        pl.when(count > nearest)(functools.partial(region, first, number))

    for g in range(KEY_VALUE_HEADS):
        result = (acc[g, :, :HEAD_SIZE] / acc[g, :, HEAD_SIZE:]).astype(bf16)
        for j in range(GROUP_SPLIT):
            for ref in (out_ref, copy_ref):
                ref[:, columns(g * GROUP_SPLIT + j, HEAD_SIZE)] = result[columns(j, tokens)]


def attend(plan, queries, blocks, steps):
    tokens = blocks[0].shape[0]
    rows = GROUP_SPLIT * tokens
    limit = VMEM_LIMIT if len(blocks) < 16 else 2 * VMEM_LIMIT
    return pl.pallas_call(
        functools.partial(attend_kernel, steps),
        out_shape=[jax.ShapeDtypeStruct((tokens, QUERY_HEADS * HEAD_SIZE), jnp.bfloat16)] * 2,
        in_specs=smem() + vmem(1 + len(blocks)),
        out_specs=vmem(2),
        scratch_shapes=[
            pltpu.VMEM((KEY_VALUE_HEADS, rows, HEAD_SIZE), jnp.float32),
            pltpu.VMEM((KEY_VALUE_HEADS, rows, 2 * HEAD_SIZE), jnp.float32),
        ],
        compiler_params=pltpu.CompilerParams(vmem_limit_bytes=limit),
        cost_estimate=pl.CostEstimate(
            flops=12_000_000_000, bytes_accessed=8 << 20, transcendentals=4 << 20
        ),
        name="attend",
    )(plan, queries, *blocks)


def output_kernel(at, attended_ref, piece_ref, out_ref):
    q_head = attended_ref.shape[1] // CHUNKS
    d = out_ref.shape[1] // CHUNKS
    low = jnp.zeros((attended_ref.shape[0], ROW_BLOCKS * 16), jnp.float32)
    for chunk in range(CHUNKS):
        down = factor(piece_ref, chunk, at, q_head)
        low += dot_nt(attended_ref[:, columns(chunk, q_head)], down)
    low = low.astype(jnp.bfloat16)
    for chunk in range(CHUNKS):
        result = adapter_scale * jnp.dot(
            low, factor(piece_ref, chunk, at + q_head, d), preferred_element_type=jnp.float32
        )
        out_ref[:, columns(chunk, d)] = result.astype(jnp.bfloat16)


def output_adapter(attended, pieces, model_width, at):
    return pl.pallas_call(
        functools.partial(output_kernel, at),
        out_shape=jax.ShapeDtypeStruct((attended.shape[0], model_width), jnp.bfloat16),
        in_specs=vmem(2),
        out_specs=vmem()[0],
        compiler_params=PARAMS,
        cost_estimate=pl.CostEstimate(
            flops=100_000_000, bytes_accessed=3 << 20, transcendentals=0
        ),
        name="output",
    )(attended, pieces)


def earlier_shards(shards):
    longest = shards // 2 + 1
    low = -(longest // 2)
    runs = (
        [i % shards for i in range(low, low + longest)],
        [i % shards for i in range(low + longest, low + shards)],
    )
    limits = (longest, shards - longest - 1)
    earlier = {}
    for run, limit in zip(runs, limits):
        for i, shard in enumerate(run):
            earlier[shard] = set(run[max(0, i - limit + 1) : i])
    return earlier


def shift_pairs(shards, shift):
    earlier = earlier_shards(shards)
    pairs = [((d - shift) % shards, d) for d in range(shards)]
    return [(s, d) for s, d in pairs if s in earlier[d] or s in earlier[d ^ 1]]


def swap_pairs(shards, shift):
    earlier = earlier_shards(shards)
    return [(d, d ^ 1) for d in range(shards) if (d - shift) % shards in earlier[d ^ 1]]


def exchange(kv, queries, shards, reach):
    shifts = range(0, reach + 1, 2)
    got = [kv] + [lax.ppermute(kv, "ctx", shift_pairs(shards, s)) for s in shifts[1:]]
    got[1:], queries = lax.optimization_barrier((got[1:], queries))
    swapped = [lax.ppermute(b, "ctx", swap_pairs(shards, s)) for s, b in zip(shifts, got)]
    blocks, steps = [kv], [(0, True)]
    for s, even, odd in zip(shifts, got, swapped):
        if s:
            blocks.append(even)
            steps.append((s, True))
        blocks.append(odd)
        steps.append((s, False))
    return blocks, steps, queries


def body(
    hidden,
    frozen_query,
    frozen_key,
    frozen_value,
    adapter_bank,
    request_shards,
    request_adapter,
    adapter_owner,
):
    shards = lax.axis_size("ctx")
    groups = lax.axis_size("groups")
    tokens, model_width = hidden.shape
    halves = 2 if groups == 2 and 2 * shards == ROW_BLOCKS * CHUNKS else 1
    own_half = lax.axis_index("groups") if halves == 2 else 0
    me = jnp.stack([lax.axis_index("ctx"), own_half]).astype(jnp.int32)
    parts = Parts(model_width, frozen_query.shape[1], frozen_key.shape[1])
    reach = shards // 2

    packed = pack(parts, halves, shards, me, adapter_bank)
    spread = lax.all_to_all(packed, "ctx", split_axis=0, concat_axis=0, tiled=True)

    tables = rope_tables(jnp.arange((reach + 1) * tokens, dtype=jnp.int32).reshape(-1, tokens))
    requests = jnp.stack([request_shards, request_adapter])[:, None]
    if halves == 2:
        theirs = lax.ppermute(requests, "groups", [(0, 1), (1, 0)])
        requests = jnp.concatenate([requests, theirs], axis=1)
    plan = make_plan(shards, reach, me, requests[0], requests[1], adapter_owner)
    spread, tables = lax.optimization_barrier((spread, tables))

    def collect(pieces):
        axes = ("groups", "ctx") if halves == 2 else "ctx"
        pieces = lax.all_to_all(pieces, axes, split_axis=0, concat_axis=0, tiled=True)
        return pieces.reshape((halves, shards) + pieces.shape[1:])[:, : ROW_BLOCKS * CHUNKS]

    kv_width, q_width, _ = parts.widths
    first, later = route(plan, spread, kv_width + q_width)
    pieces = collect(first)
    kv = make_keys_values(plan, hidden, frozen_key, frozen_value, tables, pieces)
    queries = make_queries(plan, hidden, frozen_query, tables, pieces, kv_width)
    blocks, steps, queries = exchange(kv, queries, shards, reach)
    blocks[1], later = lax.optimization_barrier((blocks[1], later))
    later = collect(later)
    attended, copy = attend(plan, queries, blocks, steps)
    return attended, output_adapter(copy, later, model_width, 0)


def solution(mesh):
    return jax.shard_map(
        body,
        mesh=mesh,
        in_specs=(
            P(("groups", "ctx"), None),
            P(("groups", "ctx"), None),
            P(("groups", "ctx"), None),
            P(("groups", "ctx"), None),
            P("ctx", None, None),
            P("groups"),
            P("groups"),
            P(),
        ),
        out_specs=(P(("groups", "ctx"), None), P(("groups", "ctx"), None)),
        check_vma=False,
    )
```

profile of v0, /device:TPU:0, one launch (start us, length us, event | category | flops | bytes accessed | tf_op | source)
XLA Modules:
  0.0 143.0 jit_solution(3099264051577430394)
XLA Ops:
  0.7 1.8 %copy-done.2 = bf16[1,64,21504]{2,1,0:T(8,128)(2,1)S(1)} copy-done((bf16[1,64,21504]{2,1,0:T(8,128)(2,1)S(1)}, bf16[1,64,21504]{2,1,0:T(8,128)(2,1)}, u32[]{:S(2)}) %copy-start.2) | copy-done | bytes 2752536
  2.5 1.8 %pack.1 = bf16[16,16,2688]{2,1,0:T(8,128)(2,1)} custom-call(s32[2]{0:T(128)S(1)} %pad_add_fusion.1.me_ref.x_ref, bf16[1,64,21504]{2,1,0:T(8,128)(2,1)S(1)} %copy-done.2), custom_call_target="tpu_custom_call" | custom-call | tf_op jit(solution)/shard_map/pack/pallas_call | solution.py:116
  4.3 7.5 %all-to-all-start = ((bf16[16,16,2688]{2,1,0:T(8,128)(2,1)}), bf16[16,16,2688]{2,1,0:T(8,128)(2,1)S(1)}, u32[]{:S(2)}, u32[]{:S(2)}) async-start(bf16[16,16,2688]{2,1,0:T(8,128)(2,1)} %pack.1), calls=%async_computation | async-start | bytes 2752512 | tf_op jit(solution)/shard_map/all_to_all | solution.py:428
  11.8 1.6 %collective-permute-start = (s32[2,1,3]{2,0,1:T(2,128)S(1)}, s32[2,1,3]{2,0,1:T(2,128)S(1)}, u32[]{:S(2)}, u32[]{:S(2)}) collective-permute-start(s32[2,1,3]{2,0,1:T(2,128)S(1)} %add_bitcast_fusion), channel_id=1, source_target_pairs={{0,16},{16,0},{1,17},{17,1},{2,18},{18,2},{3,19},{19,3},{4,20},{20... | collective-permute-start | bytes 80 | tf_op jit(solution)/shard_map/ppermute | solution.py:433
  13.4 2.1 %fusion = (f32[9,128,64]{2,1,0:T(8,128)S(1)}, f32[9,128,64]{2,1,0:T(8,128)S(1)}, f32[9,128,64]{2,1,0:T(8,128)S(1)}) fusion(f32[64]{0:T(128)S(1)} %multiply_power_fusion, f32[9,128]{1,0:T(8,128)S(1)} %add_convert_fusion), kind=kLoop, calls=%fused_computation.4 | loop fusion | flops 147456 | bytes 889600 | tf_op jit(solution)/shard_map/neg | solution.py:31
  16.5 1.4 plan.1.plan_ref
  17.9 22.4 %all-to-all-done.spread_ref = bf16[16,16,2688]{2,1,0:T(8,128)(2,1)S(1)} async-done(((bf16[16,16,2688]{2,1,0:T(8,128)(2,1)}), bf16[16,16,2688]{2,1,0:T(8,128)(2,1)S(1)}, u32[]{:S(2)}, u32[]{:S(2)}) %all-to-all-start) | async-done | bytes 1376288 | tf_op jit(solution)/shard_map/all_to_all | solution.py:428
  42.7 54.8 %all_to_all.15 = bf16[32,16,1920]{2,1,0:T(8,128)(2,1)S(1)} all-to-all(bf16[32,16,1920]{2,1,0:T(8,128)(2,1)S(1)} %get-tuple-element.19), channel_id=1, replica_groups=mesh['groups'=2,'ctx'=16] {'groups','ctx'}, dimensions={0} | all-to-all | bytes 3932160 | tf_op jit(solution)/shard_map/all_to_all | solution.py:440
  97.5 1.3 keys_values.1.refs_0_
  98.8 1.6 %collective-permute-start.5 = (bf16[128,1024]{1,0:T(8,128)(2,1)S(1)}, bf16[128,1024]{1,0:T(8,128)(2,1)S(1)}, u32[]{:S(2)}, u32[]{:S(2)}) collective-permute-start(bf16[128,1024]{1,0:T(8,128)(2,1)S(1)} %keys_values.1.refs_0_), channel_id=1, source_target_pairs={{0,1},{2,3},{6,7},{8,9},{10,11},{12,13},{14,15},{16,17},{18,19},{2... | collective-permute-start | bytes 786440 | tf_op jit(solution)/shard_map/ppermute | solution.py:397
  100.4 1.4 collective-permute-start.4
  101.8 1.4 collective-permute-start.3
  103.2 1.9 %collective-permute-start.2 = (bf16[128,1024]{1,0:T(8,128)(2,1)S(1)}, bf16[128,1024]{1,0:T(8,128)(2,1)}, u32[]{:S(2)}, u32[]{:S(2)}) collective-permute-start(bf16[128,1024]{1,0:T(8,128)(2,1)S(1)} %keys_values.1.refs_0_), channel_id=1, source_target_pairs={{12,0},{13,1},{14,2},{15,3},{0,4},{1,5},{5,9},{6,10},{7,11},{28,16... | collective-permute-start | bytes 786440 | tf_op jit(solution)/shard_map/ppermute | solution.py:395
  105.1 2.5 %collective-permute-start.1 = (bf16[128,1024]{1,0:T(8,128)(2,1)S(1)}, bf16[128,1024]{1,0:T(8,128)(2,1)}, u32[]{:S(2)}, u32[]{:S(2)}) collective-permute-start(bf16[128,1024]{1,0:T(8,128)(2,1)S(1)} %keys_values.1.refs_0_), channel_id=1, source_target_pairs={{14,0},{15,1},{0,2},{1,3},{2,4},{3,5},{5,7},{6,8},{7,9},{8,10},{9,... | collective-permute-start | bytes 786440 | tf_op jit(solution)/shard_map/ppermute | solution.py:395
  108.3 6.3 %all-to-all-start.2 = ((bf16[32,16,768]{2,1,0:T(8,128)(2,1)}), bf16[32,16,768]{2,1,0:T(8,128)(2,1)}, u32[]{:S(2)}, u32[]{:S(2)}) async-start(bf16[32,16,768]{2,1,0:T(8,128)(2,1)} %copy-done.3), calls=%async_computation.2 | async-start | bytes 1572864 | tf_op jit(solution)/shard_map/all_to_all | solution.py:440
  114.6 1.2 copy-done.1
  116.9 1.5 %queries.1 = bf16[4,512,128]{2,1,0:T(8,128)(2,1)S(1)} custom-call(s32[40]{0:T(128)S(1)} %copy-done.8, bf16[128,4096]{1,0:T(8,128)(2,1)S(1)} %copy-done.1, bf16[128,2048]{1,0:T(8,128)(2,1)S(1)} %copy-done.4, f32[9,128,128]{2,1,0:T(8,128)S(1)} %get-tuple-element.16.cos_ref, f32[9,128,128]{2,1,0:T(8,128)S(1)} %get-tuple-element.17.sin_ref, ...), custom_call_target="tpu_custom_call" | custom-call | flops 100000000 | bytes 3145728 | tf_op jit(solution)/shard_map/queries/pallas_call | solution.py:237
  118.4 4.1 %collective-permute-done.2.refs_4_ = bf16[128,1024]{1,0:T(8,128)(2,1)} collective-permute-done((bf16[128,1024]{1,0:T(8,128)(2,1)S(1)}, bf16[128,1024]{1,0:T(8,128)(2,1)}, u32[]{:S(2)}, u32[]{:S(2)}) %collective-permute-start.2) | collective-permute-done | bytes 262176 | tf_op jit(solution)/shard_map/ppermute | solution.py:395
  122.5 2.4 %collective-permute-done.1.refs_2_ = bf16[128,1024]{1,0:T(8,128)(2,1)} collective-permute-done((bf16[128,1024]{1,0:T(8,128)(2,1)S(1)}, bf16[128,1024]{1,0:T(8,128)(2,1)}, u32[]{:S(2)}, u32[]{:S(2)}) %collective-permute-start.1) | collective-permute-done | bytes 262176 | tf_op jit(solution)/shard_map/ppermute | solution.py:395
  124.9 1.9 %collective-permute-start.6 = (bf16[128,1024]{1,0:T(8,128)(2,1)}, bf16[128,1024]{1,0:T(8,128)(2,1)S(1)}, u32[]{:S(2)}, u32[]{:S(2)}) collective-permute-start(bf16[128,1024]{1,0:T(8,128)(2,1)} %collective-permute-done.1.refs_2_), channel_id=1, source_target_pairs={{0,1},{1,0},{2,3},{3,2},{5,4},{7,6},{8,9},{9,8},{10,11},{11,10},{1... | collective-permute-start | bytes 786440 | tf_op jit(solution)/shard_map/ppermute | solution.py:397
  126.8 2.4 %collective-permute-start.7 = (bf16[128,1024]{1,0:T(8,128)(2,1)}, bf16[128,1024]{1,0:T(8,128)(2,1)S(1)}, u32[]{:S(2)}, u32[]{:S(2)}) collective-permute-start(bf16[128,1024]{1,0:T(8,128)(2,1)} %collective-permute-done.2.refs_4_), channel_id=1, source_target_pairs={{0,1},{1,0},{2,3},{3,2},{5,4},{9,8},{10,11},{11,10},{16,17},{17,16... | collective-permute-start | bytes 786440 | tf_op jit(solution)/shard_map/ppermute | solution.py:397
  130.6 5.8 %attend.1 = (bf16[128,2048]{1,0:T(8,128)(2,1)}, bf16[128,2048]{1,0:T(8,128)(2,1)S(1)}) custom-call(s32[40]{0:T(128)S(1)} %copy-done.8, bf16[4,512,128]{2,1,0:T(8,128)(2,1)S(1)} %queries.1, bf16[128,1024]{1,0:T(8,128)(2,1)S(1)} %keys_values.1.refs_0_, bf16[128,1024]{1,0:T(8,128)(2,1)S(1)} %copy-done.11, bf16[128,1024]{1,0:T(8,128)(2,1)} %collective-permute-done.1.refs_2_, ...), custom_call_target="tpu_custom_call" | custom-call | flops 12000000000 | bytes 8388608 | tf_op jit(solution)/shard_map/attend/pallas_call | solution.py:321
  136.4 3.5 %all-to-all-done.2 = bf16[32,16,768]{2,1,0:T(8,128)(2,1)} async-done(((bf16[32,16,768]{2,1,0:T(8,128)(2,1)}), bf16[32,16,768]{2,1,0:T(8,128)(2,1)}, u32[]{:S(2)}, u32[]{:S(2)}) %all-to-all-start.2) | async-done | bytes 786464 | tf_op jit(solution)/shard_map/all_to_all | solution.py:440
  139.9 3.0 %output.1 = bf16[128,4096]{1,0:T(8,128)(2,1)} custom-call(bf16[128,2048]{1,0:T(8,128)(2,1)S(1)} %get-tuple-element.28.attended_ref, bf16[2,16,16,768]{3,2,1,0:T(8,128)(2,1)} %bitcast.8.piece_ref), custom_call_target="tpu_custom_call" | custom-call | flops 100000000 | bytes 3145728 | tf_op jit(solution)/shard_map/output/pallas_call | solution.py:354
  (43 shorter events, 6.5 us)
Async XLA Ops:
  0.7 1.8 %copy-start.2 = (bf16[1,64,21504]{2,1,0:T(8,128)(2,1)S(1)}, bf16[1,64,21504]{2,1,0:T(8,128)(2,1)}, u32[]{:S(2)}) copy-start(bf16[1,64,21504]{2,1,0:T(8,128)(2,1)} %bank_ref.1) | copy-start | bytes 8257540
  2.5 1.8 %copy-start.9 = (s32[2]{0:T(128)}, s32[2]{0:T(128)S(1)}, u32[]{:S(2)}) copy-start(s32[2]{0:T(128)S(1)} %pad_add_fusion.1.me_ref.x_ref) | copy-start | bytes 28
  4.3 7.5 %copy-start.12 = (s32[3]{0:T(128)S(1)}, s32[3]{0:T(128)}, u32[]{:S(2)}) copy-start(s32[3]{0:T(128)} %param.14) | copy-start | bytes 40
  4.3 7.5 %copy-start.13 = (s32[3]{0:T(128)S(1)}, s32[3]{0:T(128)}, u32[]{:S(2)}) copy-start(s32[3]{0:T(128)} %param.13) | copy-start | bytes 40
  4.3 36.1 %all-to-all-start = ((bf16[16,16,2688]{2,1,0:T(8,128)(2,1)}), bf16[16,16,2688]{2,1,0:T(8,128)(2,1)S(1)}, u32[]{:S(2)}, u32[]{:S(2)}) async-start(bf16[16,16,2688]{2,1,0:T(8,128)(2,1)} %pack.1), calls=%async_computation | async-start | bytes 2752512 | tf_op jit(solution)/shard_map/all_to_all | solution.py:428
  11.8 4.1 %collective-permute-start = (s32[2,1,3]{2,0,1:T(2,128)S(1)}, s32[2,1,3]{2,0,1:T(2,128)S(1)}, u32[]{:S(2)}, u32[]{:S(2)}) collective-permute-start(s32[2,1,3]{2,0,1:T(2,128)S(1)} %add_bitcast_fusion), channel_id=1, source_target_pairs={{0,16},{16,0},{1,17},{17,1},{2,18},{18,2},{3,19},{19,3},{4,20},{20... | collective-permute-start | bytes 80 | tf_op jit(solution)/shard_map/ppermute | solution.py:433
  41.8 0.9 copy-start.3
  42.7 54.9 %copy-start = (bf16[128,4096]{1,0:T(8,128)(2,1)S(1)}, bf16[128,4096]{1,0:T(8,128)(2,1)}, u32[]{:S(2)}) copy-start(bf16[128,4096]{1,0:T(8,128)(2,1)} %hidden_ref.3) | copy-start | bytes 3145732
  42.7 54.9 %copy-start.5 = (bf16[128,512]{1,0:T(8,128)(2,1)S(1)}, bf16[128,512]{1,0:T(8,128)(2,1)}, u32[]{:S(2)}) copy-start(bf16[128,512]{1,0:T(8,128)(2,1)} %key_ref.1) | copy-start | bytes 393220
  42.7 54.9 %copy-start.6 = (bf16[128,512]{1,0:T(8,128)(2,1)S(1)}, bf16[128,512]{1,0:T(8,128)(2,1)}, u32[]{:S(2)}) copy-start(bf16[128,512]{1,0:T(8,128)(2,1)} %value_ref.1) | copy-start | bytes 393220
  42.7 54.9 %copy-start.8 = (s32[40]{0:T(128)S(1)}, s32[40]{0:T(128)}, u32[]{:S(2)}) copy-start(s32[40]{0:T(128)} %plan.1.plan_ref) | copy-start | bytes 484
  98.8 8.7 %collective-permute-start.5 = (bf16[128,1024]{1,0:T(8,128)(2,1)S(1)}, bf16[128,1024]{1,0:T(8,128)(2,1)S(1)}, u32[]{:S(2)}, u32[]{:S(2)}) collective-permute-start(bf16[128,1024]{1,0:T(8,128)(2,1)S(1)} %keys_values.1.refs_0_), channel_id=1, source_target_pairs={{0,1},{2,3},{6,7},{8,9},{10,11},{12,13},{14,15},{16,17},{18,19},{2... | collective-permute-start | bytes 786440 | tf_op jit(solution)/shard_map/ppermute | solution.py:397
  100.4 18.0 %collective-permute-start.4 = (bf16[128,1024]{1,0:T(8,128)(2,1)S(1)}, bf16[128,1024]{1,0:T(8,128)(2,1)}, u32[]{:S(2)}, u32[]{:S(2)}) collective-permute-start(bf16[128,1024]{1,0:T(8,128)(2,1)S(1)} %keys_values.1.refs_0_), channel_id=1, source_target_pairs={{12,4},{13,5},{28,20},{29,21}} | collective-permute-start | bytes 786440 | tf_op jit(solution)/shard_map/ppermute | solution.py:395
  101.8 16.6 %collective-permute-start.3 = (bf16[128,1024]{1,0:T(8,128)(2,1)S(1)}, bf16[128,1024]{1,0:T(8,128)(2,1)}, u32[]{:S(2)}, u32[]{:S(2)}) collective-permute-start(bf16[128,1024]{1,0:T(8,128)(2,1)S(1)} %keys_values.1.refs_0_), channel_id=1, source_target_pairs={{12,2},{13,3},{14,4},{15,5},{5,11},{28,18},{29,19},{30,20},{31,21}... | collective-permute-start | bytes 786440 | tf_op jit(solution)/shard_map/ppermute | solution.py:395
  103.2 19.3 %collective-permute-start.2 = (bf16[128,1024]{1,0:T(8,128)(2,1)S(1)}, bf16[128,1024]{1,0:T(8,128)(2,1)}, u32[]{:S(2)}, u32[]{:S(2)}) collective-permute-start(bf16[128,1024]{1,0:T(8,128)(2,1)S(1)} %keys_values.1.refs_0_), channel_id=1, source_target_pairs={{12,0},{13,1},{14,2},{15,3},{0,4},{1,5},{5,9},{6,10},{7,11},{28,16... | collective-permute-start | bytes 786440 | tf_op jit(solution)/shard_map/ppermute | solution.py:395
  105.1 19.8 %collective-permute-start.1 = (bf16[128,1024]{1,0:T(8,128)(2,1)S(1)}, bf16[128,1024]{1,0:T(8,128)(2,1)}, u32[]{:S(2)}, u32[]{:S(2)}) collective-permute-start(bf16[128,1024]{1,0:T(8,128)(2,1)S(1)} %keys_values.1.refs_0_), channel_id=1, source_target_pairs={{14,0},{15,1},{0,2},{1,3},{2,4},{3,5},{5,7},{6,8},{7,9},{8,10},{9,... | collective-permute-start | bytes 786440 | tf_op jit(solution)/shard_map/ppermute | solution.py:395
  108.3 31.7 %all-to-all-start.2 = ((bf16[32,16,768]{2,1,0:T(8,128)(2,1)}), bf16[32,16,768]{2,1,0:T(8,128)(2,1)}, u32[]{:S(2)}, u32[]{:S(2)}) async-start(bf16[32,16,768]{2,1,0:T(8,128)(2,1)} %copy-done.3), calls=%async_computation.2 | async-start | bytes 1572864 | tf_op jit(solution)/shard_map/all_to_all | solution.py:440
  114.6 1.2 copy-start.1
  115.8 1.0 copy-start.4
  116.9 13.7 %copy-start.11 = (bf16[128,1024]{1,0:T(8,128)(2,1)S(1)}, bf16[128,1024]{1,0:T(8,128)(2,1)}, u32[]{:S(2)}) copy-start(bf16[128,1024]{1,0:T(8,128)(2,1)} %copy-done.10) | copy-start | bytes 786436
  124.9 5.7 %collective-permute-start.6 = (bf16[128,1024]{1,0:T(8,128)(2,1)}, bf16[128,1024]{1,0:T(8,128)(2,1)S(1)}, u32[]{:S(2)}, u32[]{:S(2)}) collective-permute-start(bf16[128,1024]{1,0:T(8,128)(2,1)} %collective-permute-done.1.refs_2_), channel_id=1, source_target_pairs={{0,1},{1,0},{2,3},{3,2},{5,4},{7,6},{8,9},{9,8},{10,11},{11,10},{1... | collective-permute-start | bytes 786440 | tf_op jit(solution)/shard_map/ppermute | solution.py:397
  126.8 3.8 %collective-permute-start.7 = (bf16[128,1024]{1,0:T(8,128)(2,1)}, bf16[128,1024]{1,0:T(8,128)(2,1)S(1)}, u32[]{:S(2)}, u32[]{:S(2)}) collective-permute-start(bf16[128,1024]{1,0:T(8,128)(2,1)} %collective-permute-done.2.refs_4_), channel_id=1, source_target_pairs={{0,1},{1,0},{2,3},{3,2},{5,4},{9,8},{10,11},{11,10},{16,17},{17,16... | collective-permute-start | bytes 786440 | tf_op jit(solution)/shard_map/ppermute | solution.py:397
  129.2 1.4 collective-permute-start.8
  129.9 0.7 collective-permute-start.9
  (2 other events, 1.3 us)
where the time goes:
time: 144 us; the launch traced here: 143 us
  blocking collectives  54.8 us (38%)
  waiting for transfers between devices  32.4 us (22%)
  starting transfers between devices  29.8 us (21%)
  Pallas kernels  15.6 us (11%)
  local copies, waits for them, and re-layouts  6.24 us (4%)
  other arithmetic  3.18 us (2%)
    all_to_all x1, blocking collectives, collect(): lax.all_to_all(pieces, axes, split_axis=0, concat_axis=0, tiled=True)  54.8 us
    all_to_all x1, waiting for transfers between devices, body(): lax.all_to_all(packed, 'ctx', split_axis=0, concat_axis=0, tiled=True)  22.4 us
    all_to_all x1, starting transfers between devices, body(): lax.all_to_all(packed, 'ctx', split_axis=0, concat_axis=0, tiled=True)  7.52 us
    ppermute x5, starting transfers between devices, exchange(): lax.ppermute(b, 'ctx', swap_pairs(shards, s))  7.22 us
    ppermute x4, starting transfers between devices, exchange(): lax.ppermute(kv, 'ctx', shift_pairs(shards, s))  7.14 us
    ppermute x4, waiting for transfers between devices, exchange(): lax.ppermute(kv, 'ctx', shift_pairs(shards, s))  6.45 us
    all_to_all x1, starting transfers between devices, collect(): lax.all_to_all(pieces, axes, split_axis=0, concat_axis=0, tiled=True)  6.32 us
    unnamed x28, local copies, waits for them, and re-layouts  6.24 us
  transfers between devices with their start and end apart: 12, of which 4 were waited for; matrix products, arithmetic and copies ran while one was open for 2% of the time, Pallas kernels for 6%

commit v1 on v0

--- a/solution.py
+++ b/solution.py
@@ -53,7 +53,7 @@
 PARAMS = pltpu.CompilerParams(vmem_limit_bytes=VMEM_LIMIT)
 
 
-OWN_INDEX, OWN_HALF, COUNT, ENTRY = 0, 1, 2, 8
+OWN_INDEX, COUNT, ENTRY = 0, 1, 8
 
 
 def layout(lengths_ref, which, shards):
@@ -73,9 +73,8 @@
     first = jnp.int32(0)
     for start in starts[1:]:
         first = jnp.where(start <= own_packed, start, first)
-    out_ref[OWN_INDEX] = own_index
-    out_ref[OWN_HALF] = own_half
-    out_ref[COUNT] = jnp.minimum(own_packed - first, reach) + 1
+    lanes = lax.broadcasted_iota(jnp.int32, out_ref.shape, 1)
+    plan = jnp.where(lanes == COUNT, jnp.minimum(own_packed - first, reach) + 1, own_index)
     for which in range(lengths_ref.shape[0]):
         starts, offset = layout(lengths_ref, which, shards)
         entries = [owner_ref[adapters_ref[which, r]] for r in range(len(starts))]
@@ -85,68 +84,74 @@
             entry = entries[0]
             for start, later in zip(starts[1:], entries[1:]):
                 entry = jnp.where(start <= packed, later, entry)
-            out_ref[at + shard] = entry
+            plan = jnp.where(lanes == at + shard, entry, plan)
+    out_ref[...] = plan
 
 
 def make_plan(shards, reach, me, lengths, adapters, owner):
     return pl.pallas_call(
         functools.partial(plan_kernel, shards, reach),
-        out_shape=jax.ShapeDtypeStruct((ENTRY + lengths.shape[0] * shards,), jnp.int32),
+        out_shape=jax.ShapeDtypeStruct((1, 128), jnp.int32),
         in_specs=smem(4),
-        out_specs=smem()[0],
+        out_specs=vmem()[0],
         name="plan",
     )(me, lengths, adapters, owner)
 
 
-def pack_kernel(parts, halves, x_ref, bank_ref, out):
-    own_half = x_ref[1]
-    for block in range(out.shape[0]):
-        piece = block % (ROW_BLOCKS * CHUNKS // halves)
-        rows = pl.ds((piece % ROW_BLOCKS) * 16, 16)
-        chunk = (piece // ROW_BLOCKS) * halves + own_half
-        at = 0
-        for first, width in parts.all:
-            start = pl.multiple_of(first + chunk * width, 128)
-            out[block, :, at : at + width] = bank_ref[0, rows, pl.ds(start, width)]
-            at += width
+def pack_kernel(parts, halves, me_ref, bank_ref, out_ref, sem):
+    own_half = me_ref[1]
+    copies = []
+    for again in range(out_ref.shape[0]):
+        for place in range(out_ref.shape[1]):
+            at = 0
+            for first, width in parts.all:
+                start = pl.multiple_of(first + (place * halves + own_half) * width, 128)
+                copies.append(
+                    pltpu.make_async_copy(
+                        bank_ref.at[:, :, pl.ds(start, width)],
+                        out_ref.at[again, place, :, :, pl.ds(at, width)],
+                        sem.at[len(copies)],
+                    )
+                )
+                at += width
+    for copy in copies:
+        copy.start()
+    for copy in copies:
+        copy.wait()
 
 
 def pack(parts, halves, shards, me, bank):
-    width = sum(parts.widths)
-    return pl.pallas_call(
+    width, places = sum(parts.widths), CHUNKS // halves
+    again = shards // (places * ROW_BLOCKS)
+    packed = pl.pallas_call(
         functools.partial(pack_kernel, parts, halves),
-        out_shape=jax.ShapeDtypeStruct((shards, 16, width), bank.dtype),
-        in_specs=smem() + vmem(),
+        out_shape=jax.ShapeDtypeStruct((again, places, ROW_BLOCKS, 16, width), bank.dtype),
+        in_specs=smem() + [pl.BlockSpec(memory_space=pl.ANY)],
         out_specs=vmem()[0],
-        compiler_params=PARAMS,
+        scratch_shapes=[pltpu.SemaphoreType.DMA((again * places * len(parts.all),))],
+        compiler_params=pltpu.CompilerParams(vmem_limit_bytes=62 * 1024 * 1024),
         name="pack",
-    )(me, bank)
+    )(me, bank.reshape(ROW_BLOCKS, 16, bank.shape[2]))
+    return packed.reshape(shards, 16, width)
 
 
 ROUTE_STEPS = 4
 
 
-def route_kernel(plan_ref, spread_ref, *outs):
-    number = outs[0].shape[0]
+def route_kernel(at, plan_ref, spread_ref, out_ref):
+    number = out_ref.shape[0]
     for i in range(number):
-        entry = plan_ref[ENTRY + pl.program_id(0) * number + i]
-        at = 0
-        for out in outs:
-            out[i] = spread_ref[entry, :, at : at + out.shape[2]]
-            at += out.shape[2]
-
-
-def route(plan, spread, first_width):
-    dests = plan.shape[0] - ENTRY
-    widths = (first_width, spread.shape[2] - first_width)
-    return pl.pallas_call(
-        route_kernel,
-        out_shape=[jax.ShapeDtypeStruct((dests, 16, w), spread.dtype) for w in widths],
+        entry = plan_ref[0, ENTRY + pl.program_id(0) * number + i]
+        out_ref[i] = spread_ref[entry, :, at : at + out_ref.shape[2]]
+
+
+def route(plan, spread, dests, at, width):
+    return pl.pallas_call(
+        functools.partial(route_kernel, at),
+        out_shape=jax.ShapeDtypeStruct((dests, 16, width), spread.dtype),
         grid=(ROUTE_STEPS,),
         in_specs=smem() + vmem(),
-        out_specs=[
-            pl.BlockSpec((dests // ROUTE_STEPS, 16, w), lambda i: (i, 0, 0)) for w in widths
-        ],
+        out_specs=pl.BlockSpec((dests // ROUTE_STEPS, 16, width), lambda i: (i, 0, 0)),
         compiler_params=PARAMS,
         name="route",
     )(plan, spread)
@@ -182,7 +187,7 @@
         low += dot_nt(hidden_ref[:, columns(chunk, d)], down)
     low = low.astype(jnp.bfloat16)
     width = 2 * key_ref.shape[1] // CHUNKS
-    own = plan_ref[COUNT] - 1
+    own = plan_ref[0, COUNT] - 1
     cosines, sines = cos_ref[own], sin_ref[own]
     for chunk in range(CHUNKS):
         is_key = chunk < CHUNKS // 2
@@ -218,7 +223,7 @@
     for chunk in range(CHUNKS):
         low += dot_nt(hidden_ref[:, columns(chunk, d)], factor(piece_ref, chunk, at, d))
     low = low.astype(jnp.bfloat16)
-    own = plan_ref[COUNT] - 1
+    own = plan_ref[0, COUNT] - 1
     cosines, sines = cos_ref[own], sin_ref[own]
     for chunk in range(CHUNKS):
         up = factor(piece_ref, chunk, at + d, width)
@@ -254,8 +259,8 @@
 
 def attend_kernel(steps, plan_ref, queries, *refs):
     blocks, (out_ref, copy_ref, high, acc) = refs[:-4], refs[-4:]
-    count = plan_ref[COUNT]
-    odd = lax.rem(plan_ref[OWN_INDEX], 2)
+    count = plan_ref[0, COUNT]
+    odd = lax.rem(plan_ref[0, OWN_INDEX], 2)
     aside = 2 * odd - 1
     steps = [s if even else s + aside for s, even in steps]
     tokens = out_ref.shape[0]
@@ -440,13 +445,14 @@
         pieces = lax.all_to_all(pieces, axes, split_axis=0, concat_axis=0, tiled=True)
         return pieces.reshape((halves, shards) + pieces.shape[1:])[:, : ROW_BLOCKS * CHUNKS]
 
-    kv_width, q_width, _ = parts.widths
-    first, later = route(plan, spread, kv_width + q_width)
-    pieces = collect(first)
+    kv_width, q_width, o_width = parts.widths
+    dests = shards * halves
+    pieces = collect(route(plan, spread, dests, 0, kv_width + q_width))
     kv = make_keys_values(plan, hidden, frozen_key, frozen_value, tables, pieces)
     queries = make_queries(plan, hidden, frozen_query, tables, pieces, kv_width)
     blocks, steps, queries = exchange(kv, queries, shards, reach)
-    blocks[1], later = lax.optimization_barrier((blocks[1], later))
+    later = route(plan, spread, dests, kv_width + q_width, o_width)
+    kv, later = lax.optimization_barrier((kv, later))
     later = collect(later)
     attended, copy = attend(plan, queries, blocks, steps)
     return attended, output_adapter(copy, later, model_width, 0)

time: 144 us -> 143 us (level)
  waiting for transfers between devices: 32.4 us -> 26.8 us
  Pallas kernels: 15.6 us -> 18.7 us
  other arithmetic: 3.18 us -> 4.72 us
    ppermute x4, waiting for transfers between devices: 6.45 us -> 2.08 us  [exchange(): lax.ppermute(kv, 'ctx', shift_pairs(shards, s))]
    pallas_call x1, Pallas kernels: 1.77 us -> 3.37 us  [pack(): pl.pallas_call(functools.partial(pack_kernel, parts, halves), out_shape=j...]
  transfers between devices with their start and end apart: 12 -> 12, of which waited for: 4 -> 3; matrix products, arithmetic and copies ran while one was open for 2% -> 3% of each run, Pallas kernels for 6% -> 7%
where the time goes in v1:
time: 143 us
  blocking collectives  54.8 us (38%)
  starting transfers between devices  30.7 us (21%)
  waiting for transfers between devices  26.8 us (19%)
  Pallas kernels  18.7 us (13%)
  local copies, waits for them, and re-layouts  5.98 us (4%)
  other arithmetic  4.72 us (3%)
    all_to_all x1, blocking collectives, collect(): lax.all_to_all(pieces, axes, split_axis=0, concat_axis=0, tiled=True)  54.8 us
    all_to_all x1, waiting for transfers between devices, body(): lax.all_to_all(packed, 'ctx', split_axis=0, concat_axis=0, tiled=True)  21.4 us
    ppermute x5, starting transfers between devices, exchange(): lax.ppermute(b, 'ctx', swap_pairs(shards, s))  7.77 us
    all_to_all x1, starting transfers between devices, body(): lax.all_to_all(packed, 'ctx', split_axis=0, concat_axis=0, tiled=True)  7.4 us
    ppermute x4, starting transfers between devices, exchange(): lax.ppermute(kv, 'ctx', shift_pairs(shards, s))  7.32 us
    all_to_all x1, starting transfers between devices, collect(): lax.all_to_all(pieces, axes, split_axis=0, concat_axis=0, tiled=True)  6.64 us
    unnamed x28, local copies, waits for them, and re-layouts  5.98 us
    pallas_call x1, Pallas kernels, attend(): pl.pallas_call(functools.partial(attend_kernel, steps), out_shape=[jax.Sh...  5.89 us
  transfers between devices with their start and end apart: 12, of which 3 were waited for; matrix products, arithmetic and copies ran while one was open for 3% of the time, Pallas kernels for 7%

profile of v1, /device:TPU:0, one launch (start us, length us, event | category | flops | bytes accessed | tf_op | source)
XLA Modules:
  0.0 142.7 jit_solution(11295406274087731834)
XLA Ops:
  1.2 3.4 %pack.1 = bf16[1,4,4,16,2688]{4,3,2,1,0:T(8,128)(2,1)} custom-call(s32[2]{0:T(128)} %pad_add_fusion.1.me_ref, bf16[4,16,21504]{2,1,0:T(8,128)(2,1)} %bitcast.15), custom_call_target="tpu_custom_call" | custom-call | tf_op jit(solution)/shard_map/pack/pallas_call | solution.py:126
  4.6 7.4 %all-to-all-start = ((bf16[16,16,2688]{2,1,0:T(8,128)(2,1)}), bf16[16,16,2688]{2,1,0:T(8,128)(2,1)S(1)}, u32[]{:S(2)}, u32[]{:S(2)}) async-start(bf16[16,16,2688]{2,1,0:T(8,128)(2,1)} %bitcast.14), calls=%async_computation | async-start | bytes 2752512 | tf_op jit(solution)/shard_map/all_to_all | solution.py:433
  12.1 1.6 %collective-permute-start = (s32[2,1,3]{2,0,1:T(2,128)S(1)}, s32[2,1,3]{2,0,1:T(2,128)S(1)}, u32[]{:S(2)}, u32[]{:S(2)}) collective-permute-start(s32[2,1,3]{2,0,1:T(2,128)S(1)} %add_bitcast_fusion), channel_id=1, source_target_pairs={{0,16},{16,0},{1,17},{17,1},{2,18},{18,2},{3,19},{19,3},{4,20},{20... | collective-permute-start | bytes 80 | tf_op jit(solution)/shard_map/ppermute | solution.py:438
  13.6 2.1 %fusion = (f32[9,128,64]{2,1,0:T(8,128)S(1)}, f32[9,128,64]{2,1,0:T(8,128)S(1)}, f32[9,128,64]{2,1,0:T(8,128)S(1)}) fusion(f32[64]{0:T(128)S(1)} %multiply_power_fusion, f32[9,128]{1,0:T(8,128)S(1)} %add_convert_fusion), kind=kLoop, calls=%fused_computation.4 | loop fusion | flops 147456 | bytes 889600 | tf_op jit(solution)/shard_map/neg | solution.py:31
  15.8 1.4 pad_maximum_fusion
  17.8 1.4 %plan.1.plan_ref = s32[1,128]{1,0:T(1,128)} custom-call(s32[2]{0:T(128)} %pad_add_fusion.1.me_ref, s32[2,3]{1,0:T(2,128)} %bitcast.17, s32[2,3]{1,0:T(2,128)} %bitcast.16, s32[16]{0:T(128)} %owner_ref.1), custom_call_target="tpu_custom_call" | custom-call | tf_op jit(solution)/shard_map/plan/pallas_call | solution.py:92
  19.2 21.4 %all-to-all-done.spread_ref = bf16[16,16,2688]{2,1,0:T(8,128)(2,1)S(1)} async-done(((bf16[16,16,2688]{2,1,0:T(8,128)(2,1)}), bf16[16,16,2688]{2,1,0:T(8,128)(2,1)S(1)}, u32[]{:S(2)}, u32[]{:S(2)}) %all-to-all-start) | async-done | bytes 1376288 | tf_op jit(solution)/shard_map/all_to_all | solution.py:433
  42.1 54.8 %all_to_all.15 = bf16[32,16,1920]{2,1,0:T(8,128)(2,1)S(1)} all-to-all(bf16[32,16,1920]{2,1,0:T(8,128)(2,1)S(1)} %route.2), channel_id=1, replica_groups=mesh['groups'=2,'ctx'=16] {'groups','ctx'}, dimensions={0} | all-to-all | bytes 3932160 | tf_op jit(solution)/shard_map/all_to_all | solution.py:445
  97.0 2.0 %keys_values.1.refs_0_ = bf16[128,1024]{1,0:T(8,128)(2,1)} custom-call(s32[1,128]{1,0:T(1,128)S(1)} %copy-done.11, bf16[128,4096]{1,0:T(8,128)(2,1)S(1)} %copy-done.4, bf16[128,512]{1,0:T(8,128)(2,1)S(1)} %copy-done.8, bf16[128,512]{1,0:T(8,128)(2,1)S(1)} %copy-done.9, f32[9,128,128]{2,1,0:T(8,128)S(1)} %copy-done, f32[9,128,128]{2,1,0:T(8,128)S(1)} %copy-done.2, ...), custom_call_target="tpu_custom_call" | custom-call | flops 150000000 | bytes 3145728 | tf_op jit(solution)/shard_map/keys_values/pallas_call | solution.py:205
  99.0 1.3 collective-permute-start.4
  100.3 1.4 collective-permute-start.3
  101.7 2.1 %collective-permute-start.2 = (bf16[128,1024]{1,0:T(8,128)(2,1)}, bf16[128,1024]{1,0:T(8,128)(2,1)}, u32[]{:S(2)}, u32[]{:S(2)}) collective-permute-start(bf16[128,1024]{1,0:T(8,128)(2,1)} %keys_values.1.refs_0_), channel_id=1, source_target_pairs={{12,0},{13,1},{14,2},{15,3},{0,4},{1,5},{5,9},{6,10},{7,11},{28,16... | collective-permute-start | bytes 786440 | tf_op jit(solution)/shard_map/ppermute | solution.py:400
  103.8 2.6 %collective-permute-start.1 = (bf16[128,1024]{1,0:T(8,128)(2,1)}, bf16[128,1024]{1,0:T(8,128)(2,1)}, u32[]{:S(2)}, u32[]{:S(2)}) collective-permute-start(bf16[128,1024]{1,0:T(8,128)(2,1)} %keys_values.1.refs_0_), channel_id=1, source_target_pairs={{14,0},{15,1},{0,2},{1,3},{2,4},{3,5},{5,7},{6,8},{7,9},{8,10},{9,... | collective-permute-start | bytes 786440 | tf_op jit(solution)/shard_map/ppermute | solution.py:400
  107.9 6.6 %all-to-all-start.2 = ((bf16[32,16,768]{2,1,0:T(8,128)(2,1)}), bf16[32,16,768]{2,1,0:T(8,128)(2,1)}, u32[]{:S(2)}, u32[]{:S(2)}) async-start(bf16[32,16,768]{2,1,0:T(8,128)(2,1)} %copy-done.6), calls=%async_computation.2 | async-start | bytes 1572864 | tf_op jit(solution)/shard_map/all_to_all | solution.py:445
  114.6 2.1 %collective-permute-start.5 = (bf16[128,1024]{1,0:T(8,128)(2,1)}, bf16[128,1024]{1,0:T(8,128)(2,1)S(1)}, u32[]{:S(2)}, u32[]{:S(2)}) collective-permute-start(bf16[128,1024]{1,0:T(8,128)(2,1)} %keys_values.1.refs_0_), channel_id=1, source_target_pairs={{0,1},{2,3},{6,7},{8,9},{10,11},{12,13},{14,15},{16,17},{18,19},{2... | collective-permute-start | bytes 786440 | tf_op jit(solution)/shard_map/ppermute | solution.py:402
  117.8 1.1 copy-done.3
  118.8 1.2 copy-done.5
  121.1 1.5 %queries.1 = bf16[4,512,128]{2,1,0:T(8,128)(2,1)S(1)} custom-call(s32[1,128]{1,0:T(1,128)S(1)} %copy-done.11, bf16[128,4096]{1,0:T(8,128)(2,1)S(1)} %copy-done.5, bf16[128,2048]{1,0:T(8,128)(2,1)S(1)} %copy-done.7, f32[9,128,128]{2,1,0:T(8,128)S(1)} %copy-done.1, f32[9,128,128]{2,1,0:T(8,128)S(1)} %copy-done.3, bf16[2,16,16,1920]{3,2,1,0:T(8,128)(2,1)S(1)} %bitcast.13), custom_call_target="tpu_custom_call" | custom-call | flops 100000000 | bytes 3145728 | tf_op jit(solution)/shard_map/queries/pallas_call | solution.py:242
  122.6 2.1 %collective-permute-done.1.refs_2_ = bf16[128,1024]{1,0:T(8,128)(2,1)} collective-permute-done((bf16[128,1024]{1,0:T(8,128)(2,1)}, bf16[128,1024]{1,0:T(8,128)(2,1)}, u32[]{:S(2)}, u32[]{:S(2)}) %collective-permute-start.1) | collective-permute-done | bytes 262176 | tf_op jit(solution)/shard_map/ppermute | solution.py:400
  124.7 1.9 %collective-permute-start.6 = (bf16[128,1024]{1,0:T(8,128)(2,1)}, bf16[128,1024]{1,0:T(8,128)(2,1)S(1)}, u32[]{:S(2)}, u32[]{:S(2)}) collective-permute-start(bf16[128,1024]{1,0:T(8,128)(2,1)} %collective-permute-done.1.refs_2_), channel_id=1, source_target_pairs={{0,1},{1,0},{2,3},{3,2},{5,4},{7,6},{8,9},{9,8},{10,11},{11,10},{1... | collective-permute-start | bytes 786440 | tf_op jit(solution)/shard_map/ppermute | solution.py:402
  126.6 2.4 %collective-permute-start.7 = (bf16[128,1024]{1,0:T(8,128)(2,1)}, bf16[128,1024]{1,0:T(8,128)(2,1)S(1)}, u32[]{:S(2)}, u32[]{:S(2)}) collective-permute-start(bf16[128,1024]{1,0:T(8,128)(2,1)} %collective-permute-done.2.refs_4_), channel_id=1, source_target_pairs={{0,1},{1,0},{2,3},{3,2},{5,4},{9,8},{10,11},{11,10},{16,17},{17,16... | collective-permute-start | bytes 786440 | tf_op jit(solution)/shard_map/ppermute | solution.py:402
  130.5 5.9 %attend.1 = (bf16[128,2048]{1,0:T(8,128)(2,1)}, bf16[128,2048]{1,0:T(8,128)(2,1)S(1)}) custom-call(s32[1,128]{1,0:T(1,128)S(1)} %copy-done.11, bf16[4,512,128]{2,1,0:T(8,128)(2,1)S(1)} %queries.1, bf16[128,1024]{1,0:T(8,128)(2,1)} %keys_values.1.refs_0_, bf16[128,1024]{1,0:T(8,128)(2,1)S(1)} %collective-permute-done.5.refs_1_, ...), custom_call_target="tpu_custom_call" | custom-call | flops 12000000000 | bytes 8388608 | tf_op jit(solution)/shard_map/attend/pallas_call | solution.py:326
  136.4 3.3 %all-to-all-done.2 = bf16[32,16,768]{2,1,0:T(8,128)(2,1)} async-done(((bf16[32,16,768]{2,1,0:T(8,128)(2,1)}), bf16[32,16,768]{2,1,0:T(8,128)(2,1)}, u32[]{:S(2)}, u32[]{:S(2)}) %all-to-all-start.2) | async-done | bytes 786464 | tf_op jit(solution)/shard_map/all_to_all | solution.py:445
  139.6 3.0 %output.1 = bf16[128,4096]{1,0:T(8,128)(2,1)} custom-call(bf16[128,2048]{1,0:T(8,128)(2,1)S(1)} %get-tuple-element.22.attended_ref, bf16[2,16,16,768]{3,2,1,0:T(8,128)(2,1)} %bitcast.10.piece_ref), custom_call_target="tpu_custom_call" | custom-call | flops 100000000 | bytes 3145728 | tf_op jit(solution)/shard_map/output/pallas_call | solution.py:359
  (44 shorter events, 7.7 us)
Async XLA Ops:
  4.6 7.4 %copy-start.12 = (s32[3]{0:T(128)S(1)}, s32[3]{0:T(128)}, u32[]{:S(2)}) copy-start(s32[3]{0:T(128)} %param.14) | copy-start | bytes 40
  4.6 7.4 %copy-start.13 = (s32[3]{0:T(128)S(1)}, s32[3]{0:T(128)}, u32[]{:S(2)}) copy-start(s32[3]{0:T(128)} %param.13) | copy-start | bytes 40
  4.6 36.0 %all-to-all-start = ((bf16[16,16,2688]{2,1,0:T(8,128)(2,1)}), bf16[16,16,2688]{2,1,0:T(8,128)(2,1)S(1)}, u32[]{:S(2)}, u32[]{:S(2)}) async-start(bf16[16,16,2688]{2,1,0:T(8,128)(2,1)} %bitcast.14), calls=%async_computation | async-start | bytes 2752512 | tf_op jit(solution)/shard_map/all_to_all | solution.py:433
  12.1 5.1 %collective-permute-start = (s32[2,1,3]{2,0,1:T(2,128)S(1)}, s32[2,1,3]{2,0,1:T(2,128)S(1)}, u32[]{:S(2)}, u32[]{:S(2)}) collective-permute-start(s32[2,1,3]{2,0,1:T(2,128)S(1)} %add_bitcast_fusion), channel_id=1, source_target_pairs={{0,16},{16,0},{1,17},{17,1},{2,18},{18,2},{3,19},{19,3},{4,20},{20... | collective-permute-start | bytes 80 | tf_op jit(solution)/shard_map/ppermute | solution.py:438
  42.0 54.9 %copy-start = (f32[9,128,128]{2,1,0:T(8,128)S(1)}, f32[9,128,128]{2,1,0:T(8,128)}, u32[]{:S(2)}) copy-start(f32[9,128,128]{2,1,0:T(8,128)} %get-tuple-element.13.cos_ref) | copy-start | bytes 1769476
  42.1 54.9 %copy-start.2 = (f32[9,128,128]{2,1,0:T(8,128)S(1)}, f32[9,128,128]{2,1,0:T(8,128)}, u32[]{:S(2)}) copy-start(f32[9,128,128]{2,1,0:T(8,128)} %get-tuple-element.14.sin_ref) | copy-start | bytes 1769476
  42.1 54.9 %copy-start.4 = (bf16[128,4096]{1,0:T(8,128)(2,1)S(1)}, bf16[128,4096]{1,0:T(8,128)(2,1)}, u32[]{:S(2)}) copy-start(bf16[128,4096]{1,0:T(8,128)(2,1)} %hidden_ref.3) | copy-start | bytes 3145732
  42.1 54.9 %copy-start.8 = (bf16[128,512]{1,0:T(8,128)(2,1)S(1)}, bf16[128,512]{1,0:T(8,128)(2,1)}, u32[]{:S(2)}) copy-start(bf16[128,512]{1,0:T(8,128)(2,1)} %key_ref.1) | copy-start | bytes 393220
  42.1 54.9 %copy-start.9 = (bf16[128,512]{1,0:T(8,128)(2,1)S(1)}, bf16[128,512]{1,0:T(8,128)(2,1)}, u32[]{:S(2)}) copy-start(bf16[128,512]{1,0:T(8,128)(2,1)} %value_ref.1) | copy-start | bytes 393220
  42.1 54.9 %copy-start.11 = (s32[1,128]{1,0:T(1,128)S(1)}, s32[1,128]{1,0:T(1,128)}, u32[]{:S(2)}) copy-start(s32[1,128]{1,0:T(1,128)} %plan.1.plan_ref) | copy-start | bytes 1540
  99.0 23.6 %collective-permute-start.4 = (bf16[128,1024]{1,0:T(8,128)(2,1)}, bf16[128,1024]{1,0:T(8,128)(2,1)}, u32[]{:S(2)}, u32[]{:S(2)}) collective-permute-start(bf16[128,1024]{1,0:T(8,128)(2,1)} %keys_values.1.refs_0_), channel_id=1, source_target_pairs={{12,4},{13,5},{28,20},{29,21}} | collective-permute-start | bytes 786440 | tf_op jit(solution)/shard_map/ppermute | solution.py:400
  100.3 22.3 %collective-permute-start.3 = (bf16[128,1024]{1,0:T(8,128)(2,1)}, bf16[128,1024]{1,0:T(8,128)(2,1)}, u32[]{:S(2)}, u32[]{:S(2)}) collective-permute-start(bf16[128,1024]{1,0:T(8,128)(2,1)} %keys_values.1.refs_0_), channel_id=1, source_target_pairs={{12,2},{13,3},{14,4},{15,5},{5,11},{28,18},{29,19},{30,20},{31,21}... | collective-permute-start | bytes 786440 | tf_op jit(solution)/shard_map/ppermute | solution.py:400
  101.7 20.9 %collective-permute-start.2 = (bf16[128,1024]{1,0:T(8,128)(2,1)}, bf16[128,1024]{1,0:T(8,128)(2,1)}, u32[]{:S(2)}, u32[]{:S(2)}) collective-permute-start(bf16[128,1024]{1,0:T(8,128)(2,1)} %keys_values.1.refs_0_), channel_id=1, source_target_pairs={{12,0},{13,1},{14,2},{15,3},{0,4},{1,5},{5,9},{6,10},{7,11},{28,16... | collective-permute-start | bytes 786440 | tf_op jit(solution)/shard_map/ppermute | solution.py:400
  103.8 20.9 %collective-permute-start.1 = (bf16[128,1024]{1,0:T(8,128)(2,1)}, bf16[128,1024]{1,0:T(8,128)(2,1)}, u32[]{:S(2)}, u32[]{:S(2)}) collective-permute-start(bf16[128,1024]{1,0:T(8,128)(2,1)} %keys_values.1.refs_0_), channel_id=1, source_target_pairs={{14,0},{15,1},{0,2},{1,3},{2,4},{3,5},{5,7},{6,8},{7,9},{8,10},{9,... | collective-permute-start | bytes 786440 | tf_op jit(solution)/shard_map/ppermute | solution.py:400
  107.9 31.7 %all-to-all-start.2 = ((bf16[32,16,768]{2,1,0:T(8,128)(2,1)}), bf16[32,16,768]{2,1,0:T(8,128)(2,1)}, u32[]{:S(2)}, u32[]{:S(2)}) async-start(bf16[32,16,768]{2,1,0:T(8,128)(2,1)} %copy-done.6), calls=%async_computation.2 | async-start | bytes 1572864 | tf_op jit(solution)/shard_map/all_to_all | solution.py:445
  114.6 15.8 %collective-permute-start.5 = (bf16[128,1024]{1,0:T(8,128)(2,1)}, bf16[128,1024]{1,0:T(8,128)(2,1)S(1)}, u32[]{:S(2)}, u32[]{:S(2)}) collective-permute-start(bf16[128,1024]{1,0:T(8,128)(2,1)} %keys_values.1.refs_0_), channel_id=1, source_target_pairs={{0,1},{2,3},{6,7},{8,9},{10,11},{12,13},{14,15},{16,17},{18,19},{2... | collective-permute-start | bytes 786440 | tf_op jit(solution)/shard_map/ppermute | solution.py:402
  116.7 1.1 copy-start.1
  117.8 1.1 copy-start.3
  118.8 1.2 copy-start.5
  120.0 1.0 copy-start.7
  124.7 5.7 %collective-permute-start.6 = (bf16[128,1024]{1,0:T(8,128)(2,1)}, bf16[128,1024]{1,0:T(8,128)(2,1)S(1)}, u32[]{:S(2)}, u32[]{:S(2)}) collective-permute-start(bf16[128,1024]{1,0:T(8,128)(2,1)} %collective-permute-done.1.refs_2_), channel_id=1, source_target_pairs={{0,1},{1,0},{2,3},{3,2},{5,4},{7,6},{8,9},{9,8},{10,11},{11,10},{1... | collective-permute-start | bytes 786440 | tf_op jit(solution)/shard_map/ppermute | solution.py:402
  126.6 3.8 %collective-permute-start.7 = (bf16[128,1024]{1,0:T(8,128)(2,1)}, bf16[128,1024]{1,0:T(8,128)(2,1)S(1)}, u32[]{:S(2)}, u32[]{:S(2)}) collective-permute-start(bf16[128,1024]{1,0:T(8,128)(2,1)} %collective-permute-done.2.refs_4_), channel_id=1, source_target_pairs={{0,1},{1,0},{2,3},{3,2},{5,4},{9,8},{10,11},{11,10},{16,17},{17,16... | collective-permute-start | bytes 786440 | tf_op jit(solution)/shard_map/ppermute | solution.py:402
  129.0 1.4 collective-permute-start.8
  129.7 0.7 collective-permute-start.9
  (2 other events, 1.6 us)

commit v2 on v1

--- a/solution.py
+++ b/solution.py
@@ -98,40 +98,55 @@
     )(me, lengths, adapters, owner)
 
 
-def pack_kernel(parts, halves, me_ref, bank_ref, out_ref, sem):
-    own_half = me_ref[1]
-    copies = []
-    for again in range(out_ref.shape[0]):
-        for place in range(out_ref.shape[1]):
-            at = 0
-            for first, width in parts.all:
-                start = pl.multiple_of(first + (place * halves + own_half) * width, 128)
-                copies.append(
-                    pltpu.make_async_copy(
-                        bank_ref.at[:, :, pl.ds(start, width)],
-                        out_ref.at[again, place, :, :, pl.ds(at, width)],
-                        sem.at[len(copies)],
-                    )
+def pack_kernel(parts, halves, bank_ref, out_ref, held, in_sem, out_sem):
+    own_half = lax.axis_index("groups") if halves == 2 else 0
+    takes, gives = [], []
+    for place in range(held.shape[0]):
+        at = 0
+        for index, (first, width) in enumerate(parts.all):
+            start = pl.multiple_of(first + (place * halves + own_half) * width, 128)
+            takes.append(
+                pltpu.make_async_copy(
+                    bank_ref.at[:, :, pl.ds(start, width)],
+                    held.at[place, :, :, pl.ds(at, width)],
+                    in_sem.at[place, index],
                 )
-                at += width
-    for copy in copies:
+            )
+            at += width
+        gives += [
+            pltpu.make_async_copy(
+                held.at[place], out_ref.at[again, place], out_sem.at[again, place]
+            )
+            for again in range(out_ref.shape[0])
+        ]
+    for copy in takes:
         copy.start()
-    for copy in copies:
+    each, again = len(parts.all), out_ref.shape[0]
+    for place in range(held.shape[0]):
+        for copy in takes[place * each : (place + 1) * each]:
+            copy.wait()
+        for copy in gives[place * again : (place + 1) * again]:
+            copy.start()
+    for copy in gives:
         copy.wait()
 
 
-def pack(parts, halves, shards, me, bank):
+def pack(parts, halves, shards, bank):
     width, places = sum(parts.widths), CHUNKS // halves
     again = shards // (places * ROW_BLOCKS)
     packed = pl.pallas_call(
         functools.partial(pack_kernel, parts, halves),
         out_shape=jax.ShapeDtypeStruct((again, places, ROW_BLOCKS, 16, width), bank.dtype),
-        in_specs=smem() + [pl.BlockSpec(memory_space=pl.ANY)],
-        out_specs=vmem()[0],
-        scratch_shapes=[pltpu.SemaphoreType.DMA((again * places * len(parts.all),))],
+        in_specs=[pl.BlockSpec(memory_space=pl.ANY)],
+        out_specs=pl.BlockSpec(memory_space=pl.ANY),
+        scratch_shapes=[
+            pltpu.VMEM((places, ROW_BLOCKS, 16, width), bank.dtype),
+            pltpu.SemaphoreType.DMA((places, len(parts.all))),
+            pltpu.SemaphoreType.DMA((again, places)),
+        ],
         compiler_params=pltpu.CompilerParams(vmem_limit_bytes=62 * 1024 * 1024),
         name="pack",
-    )(me, bank.reshape(ROW_BLOCKS, 16, bank.shape[2]))
+    )(bank.reshape(ROW_BLOCKS, 16, bank.shape[2]))
     return packed.reshape(shards, 16, width)
 
 
@@ -176,7 +191,7 @@
     return x * cosines + pltpu.roll(x, HEAD_SIZE // 2, 1) * sines
 
 
-def kv_kernel(plan_ref, hidden_ref, key_ref, value_ref, cos_ref, sin_ref, piece_ref, out_ref):
+def kv_kernel(hidden_ref, key_ref, value_ref, cos_ref, sin_ref, piece_ref, out_ref):
     d = hidden_ref.shape[1] // CHUNKS
     rank = ROW_BLOCKS * 16
     low = jnp.zeros((hidden_ref.shape[0], 2 * rank), jnp.float32)
@@ -187,8 +202,7 @@
         low += dot_nt(hidden_ref[:, columns(chunk, d)], down)
     low = low.astype(jnp.bfloat16)
     width = 2 * key_ref.shape[1] // CHUNKS
-    own = plan_ref[0, COUNT] - 1
-    cosines, sines = cos_ref[own], sin_ref[own]
+    cosines, sines = cos_ref[...], sin_ref[...]
     for chunk in range(CHUNKS):
         is_key = chunk < CHUNKS // 2
         up = factor(piece_ref, chunk, 2 * d, width)
@@ -201,21 +215,21 @@
         out_ref[:, columns(chunk, width)] = result.astype(jnp.bfloat16)
 
 
-def make_keys_values(plan, hidden, key, value, tables, pieces):
+def make_keys_values(hidden, key, value, tables, pieces):
     return pl.pallas_call(
         kv_kernel,
         out_shape=jax.ShapeDtypeStruct((key.shape[0], 2 * key.shape[1]), jnp.bfloat16),
-        in_specs=smem() + vmem(6),
+        in_specs=vmem(6),
         out_specs=vmem()[0],
         compiler_params=PARAMS,
         cost_estimate=pl.CostEstimate(
             flops=150_000_000, bytes_accessed=3 << 20, transcendentals=0
         ),
         name="keys_values",
-    )(plan, hidden, key, value, *tables, pieces)
-
-
-def query_kernel(at, plan_ref, hidden_ref, query_ref, cos_ref, sin_ref, piece_ref, out_ref):
+    )(hidden, key, value, *tables, pieces)
+
+
+def query_kernel(at, hidden_ref, query_ref, cos_ref, sin_ref, piece_ref, out_ref):
     tokens = query_ref.shape[0]
     d = hidden_ref.shape[1] // CHUNKS
     width = query_ref.shape[1] // CHUNKS
@@ -223,8 +237,7 @@
     for chunk in range(CHUNKS):
         low += dot_nt(hidden_ref[:, columns(chunk, d)], factor(piece_ref, chunk, at, d))
     low = low.astype(jnp.bfloat16)
-    own = plan_ref[0, COUNT] - 1
-    cosines, sines = cos_ref[own], sin_ref[own]
+    cosines, sines = cos_ref[...], sin_ref[...]
     for chunk in range(CHUNKS):
         up = factor(piece_ref, chunk, at + d, width)
         update = jnp.dot(low, up, preferred_element_type=jnp.float32)
@@ -237,21 +250,21 @@
             )
 
 
-def make_queries(plan, hidden, query, tables, pieces, at):
+def make_queries(hidden, query, tables, pieces, at):
     tokens = hidden.shape[0]
     return pl.pallas_call(
         functools.partial(query_kernel, at),
         out_shape=jax.ShapeDtypeStruct(
             (KEY_VALUE_HEADS, GROUP_SPLIT * tokens, HEAD_SIZE), jnp.bfloat16
         ),
-        in_specs=smem() + vmem(5),
+        in_specs=vmem(5),
         out_specs=vmem()[0],
         compiler_params=PARAMS,
         cost_estimate=pl.CostEstimate(
             flops=100_000_000, bytes_accessed=3 << 20, transcendentals=0
         ),
         name="queries",
-    )(plan, hidden, query, *tables, pieces)
+    )(hidden, query, *tables, pieces)
 
 
 REGION = 5
@@ -340,27 +353,58 @@
     )(plan, queries, *blocks)
 
 
-def output_kernel(at, attended_ref, piece_ref, out_ref):
-    q_head = attended_ref.shape[1] // CHUNKS
-    d = out_ref.shape[1] // CHUNKS
+def output_kernel(attended_ref, piece_ref, out_ref, down, up, held, in_sem, out_sem):
+    q_head, d = down.shape[3], up.shape[3]
+    places = down.shape[1]
+    halves = down.shape[0]
+
+    def take(copy, at, half, index):
+        source = piece_ref.at[half, pl.ds(0, places), :, pl.ds(at, copy.shape[3])]
+        return pltpu.make_async_copy(source, copy.at[half], in_sem.at[index, half])
+
+    takes = [take(down, 0, h, 0) for h in range(halves)]
+    takes_up = [take(up, q_head, h, 1) for h in range(halves)]
+    for copy in takes + takes_up:
+        copy.start()
+    for copy in takes:
+        copy.wait()
     low = jnp.zeros((attended_ref.shape[0], ROW_BLOCKS * 16), jnp.float32)
     for chunk in range(CHUNKS):
-        down = factor(piece_ref, chunk, at, q_head)
-        low += dot_nt(attended_ref[:, columns(chunk, q_head)], down)
+        low += dot_nt(attended_ref[:, columns(chunk, q_head)], factor(down, chunk, 0, q_head))
     low = low.astype(jnp.bfloat16)
+    for copy in takes_up:
+        copy.wait()
+    gives = []
     for chunk in range(CHUNKS):
         result = adapter_scale * jnp.dot(
-            low, factor(piece_ref, chunk, at + q_head, d), preferred_element_type=jnp.float32
+            low, factor(up, chunk, 0, d), preferred_element_type=jnp.float32
         )
-        out_ref[:, columns(chunk, d)] = result.astype(jnp.bfloat16)
-
-
-def output_adapter(attended, pieces, model_width, at):
+        at = pl.ds(chunk * d, d)
+        held[:, at] = result.astype(jnp.bfloat16)
+        gives.append(
+            pltpu.make_async_copy(held.at[:, at], out_ref.at[:, at], out_sem.at[chunk])
+        )
+        gives[-1].start()
+    for copy in gives:
+        copy.wait()
+
+
+def output_adapter(attended, pieces, model_width):
+    tokens, query_width = attended.shape
+    halves, places = pieces.shape[0], pieces.shape[1]
+    any_space = pl.BlockSpec(memory_space=pl.ANY)
     return pl.pallas_call(
-        functools.partial(output_kernel, at),
-        out_shape=jax.ShapeDtypeStruct((attended.shape[0], model_width), jnp.bfloat16),
-        in_specs=vmem(2),
-        out_specs=vmem()[0],
+        output_kernel,
+        out_shape=jax.ShapeDtypeStruct((tokens, model_width), jnp.bfloat16),
+        in_specs=vmem() + [any_space],
+        out_specs=any_space,
+        scratch_shapes=[
+            pltpu.VMEM((halves, places, 16, query_width // CHUNKS), jnp.bfloat16),
+            pltpu.VMEM((halves, places, 16, model_width // CHUNKS), jnp.bfloat16),
+            pltpu.VMEM((tokens, model_width), jnp.bfloat16),
+            pltpu.SemaphoreType.DMA((2, halves)),
+            pltpu.SemaphoreType.DMA((CHUNKS,)),
+        ],
         compiler_params=PARAMS,
         cost_estimate=pl.CostEstimate(
             flops=100_000_000, bytes_accessed=3 << 20, transcendentals=0
@@ -429,15 +473,16 @@
     parts = Parts(model_width, frozen_query.shape[1], frozen_key.shape[1])
     reach = shards // 2
 
-    packed = pack(parts, halves, shards, me, adapter_bank)
+    packed = pack(parts, halves, shards, adapter_bank)
     spread = lax.all_to_all(packed, "ctx", split_axis=0, concat_axis=0, tiled=True)
 
-    tables = rope_tables(jnp.arange((reach + 1) * tokens, dtype=jnp.int32).reshape(-1, tokens))
     requests = jnp.stack([request_shards, request_adapter])[:, None]
     if halves == 2:
         theirs = lax.ppermute(requests, "groups", [(0, 1), (1, 0)])
         requests = jnp.concatenate([requests, theirs], axis=1)
     plan = make_plan(shards, reach, me, requests[0], requests[1], adapter_owner)
+    positions = (plan[0, COUNT] - 1) * tokens + jnp.arange(tokens, dtype=jnp.int32)
+    tables = rope_tables(positions)
     spread, tables = lax.optimization_barrier((spread, tables))
 
     def collect(pieces):
@@ -448,14 +493,14 @@
     kv_width, q_width, o_width = parts.widths
     dests = shards * halves
     pieces = collect(route(plan, spread, dests, 0, kv_width + q_width))
-    kv = make_keys_values(plan, hidden, frozen_key, frozen_value, tables, pieces)
-    queries = make_queries(plan, hidden, frozen_query, tables, pieces, kv_width)
+    kv = make_keys_values(hidden, frozen_key, frozen_value, tables, pieces)
+    queries = make_queries(hidden, frozen_query, tables, pieces, kv_width)
     blocks, steps, queries = exchange(kv, queries, shards, reach)
     later = route(plan, spread, dests, kv_width + q_width, o_width)
     kv, later = lax.optimization_barrier((kv, later))
     later = collect(later)
     attended, copy = attend(plan, queries, blocks, steps)
-    return attended, output_adapter(copy, later, model_width, 0)
+    return attended, output_adapter(copy, later, model_width)
 
 
 def solution(mesh):

time: 143 us -> 140 us (0.979)
  Pallas kernels: 18.7 us -> 15.3 us
  waiting for transfers between devices: 26.8 us -> 30.2 us
  other arithmetic: 4.72 us -> 1.67 us
    ppermute x4, waiting for transfers between devices: 2.08 us -> 4.8 us  [exchange(): lax.ppermute(kv, 'ctx', shift_pairs(shards, s))]
    unnamed x28 -> x20, local copies, waits for them, and re-layouts: 5.98 us -> 3.78 us
    neg x1, other arithmetic: 2.13 us -> 0.31 us  [rope_tables(): -sines]
  transfers between devices with their start and end apart: 12 -> 12, of which waited for: 3 -> 5; matrix products, arithmetic and copies ran while one was open for 3% -> 2% of each run, Pallas kernels for 7% -> 6%
where the time goes in v2:
time: 140 us; the launch traced here: 139 us
  blocking collectives  54.8 us (39%)
  starting transfers between devices  30.6 us (22%)
  waiting for transfers between devices  30.2 us (22%)
  Pallas kernels  15.3 us (11%)
  local copies, waits for them, and re-layouts  4.97 us (4%)
  other arithmetic  1.67 us (1%)
  between operations  1.56 us (1%)
    all_to_all x1, blocking collectives, collect(): lax.all_to_all(pieces, axes, split_axis=0, concat_axis=0, tiled=True)  54.8 us
    all_to_all x1, waiting for transfers between devices, body(): lax.all_to_all(packed, 'ctx', split_axis=0, concat_axis=0, tiled=True)  20.7 us
    ppermute x5, starting transfers between devices, exchange(): lax.ppermute(b, 'ctx', swap_pairs(shards, s))  7.84 us
    all_to_all x1, starting transfers between devices, body(): lax.all_to_all(packed, 'ctx', split_axis=0, concat_axis=0, tiled=True)  7.4 us
    ppermute x4, starting transfers between devices, exchange(): lax.ppermute(kv, 'ctx', shift_pairs(shards, s))  7.33 us
    all_to_all x1, starting transfers between devices, collect(): lax.all_to_all(pieces, axes, split_axis=0, concat_axis=0, tiled=True)  6.5 us
    pallas_call x1, Pallas kernels, attend(): pl.pallas_call(functools.partial(attend_kernel, steps), out_shape=[jax.Sh...  5.76 us
    ppermute x4, waiting for transfers between devices, exchange(): lax.ppermute(kv, 'ctx', shift_pairs(shards, s))  4.8 us
  transfers between devices with their start and end apart: 12, of which 5 were waited for; matrix products, arithmetic and copies ran while one was open for 2% of the time, Pallas kernels for 6%

profile of v2, /device:TPU:0, one launch (start us, length us, event | category | flops | bytes accessed | tf_op | source)
XLA Modules:
  0.0 139.1 jit_solution(6738897738540613881)
XLA Ops:
  0.6 2.4 %pack.1 = bf16[1,4,4,16,2688]{4,3,2,1,0:T(8,128)(2,1)} custom-call(bf16[4,16,21504]{2,1,0:T(8,128)(2,1)} %bitcast.17), custom_call_target="tpu_custom_call" | custom-call | tf_op jit(solution)/shard_map/pack/pallas_call | solution.py:137
  3.1 7.4 %all-to-all-start = ((bf16[16,16,2688]{2,1,0:T(8,128)(2,1)}), bf16[16,16,2688]{2,1,0:T(8,128)(2,1)S(1)}, u32[]{:S(2)}, u32[]{:S(2)}) async-start(bf16[16,16,2688]{2,1,0:T(8,128)(2,1)} %bitcast.16), calls=%async_computation | async-start | bytes 2752512 | tf_op jit(solution)/shard_map/all_to_all | solution.py:477
  10.5 1.6 %collective-permute-start = (s32[2,1,3]{2,0,1:T(2,128)S(1)}, s32[2,1,3]{2,0,1:T(2,128)S(1)}, u32[]{:S(2)}, u32[]{:S(2)}) collective-permute-start(s32[2,1,3]{2,0,1:T(2,128)S(1)} %add_bitcast_fusion), channel_id=1, source_target_pairs={{0,16},{16,0},{1,17},{17,1},{2,18},{18,2},{3,19},{19,3},{4,20},{20... | collective-permute-start | bytes 80 | tf_op jit(solution)/shard_map/ppermute | solution.py:481
  12.8 1.4 %collective-permute-done = s32[2,1,3]{2,0,1:T(2,128)S(1)} collective-permute-done((s32[2,1,3]{2,0,1:T(2,128)S(1)}, s32[2,1,3]{2,0,1:T(2,128)S(1)}, u32[]{:S(2)}, u32[]{:S(2)}) %collective-permute-start) | collective-permute-done | bytes 56 | tf_op jit(solution)/shard_map/ppermute | solution.py:481
  14.8 1.4 plan.1.plan_ref
  16.1 1.2 slice.11
  18.4 20.7 %all-to-all-done.spread_ref = bf16[16,16,2688]{2,1,0:T(8,128)(2,1)S(1)} async-done(((bf16[16,16,2688]{2,1,0:T(8,128)(2,1)}), bf16[16,16,2688]{2,1,0:T(8,128)(2,1)S(1)}, u32[]{:S(2)}, u32[]{:S(2)}) %all-to-all-start) | async-done | bytes 1376288 | tf_op jit(solution)/shard_map/all_to_all | solution.py:477
  40.5 54.8 %all_to_all.15 = bf16[32,16,1920]{2,1,0:T(8,128)(2,1)S(1)} all-to-all(bf16[32,16,1920]{2,1,0:T(8,128)(2,1)S(1)} %route.2), channel_id=1, replica_groups=mesh['groups'=2,'ctx'=16] {'groups','ctx'}, dimensions={0} | all-to-all | bytes 3932160 | tf_op jit(solution)/shard_map/all_to_all | solution.py:490
  95.3 1.5 %keys_values.1.refs_0_ = bf16[128,1024]{1,0:T(8,128)(2,1)} custom-call(bf16[128,4096]{1,0:T(8,128)(2,1)S(1)} %copy-done, bf16[128,512]{1,0:T(8,128)(2,1)S(1)} %copy-done.4, bf16[128,512]{1,0:T(8,128)(2,1)S(1)} %copy-done.5, f32[128,128]{1,0:T(8,128)S(1)} %get-tuple-element.13.cos_ref, f32[128,128]{1,0:T(8,128)S(1)} %get-tuple-element.14.sin_ref, ...), custom_call_target="tpu_custom_call" | custom-call | flops 150000000 | bytes 3145728 | tf_op jit(solution)/shard_map/keys_values/pallas_call | solution.py:219
  96.8 1.4 collective-permute-start.4
  98.2 1.4 collective-permute-start.3
  99.5 2.1 %collective-permute-start.2 = (bf16[128,1024]{1,0:T(8,128)(2,1)}, bf16[128,1024]{1,0:T(8,128)(2,1)}, u32[]{:S(2)}, u32[]{:S(2)}) collective-permute-start(bf16[128,1024]{1,0:T(8,128)(2,1)} %keys_values.1.refs_0_), channel_id=1, source_target_pairs={{12,0},{13,1},{14,2},{15,3},{0,4},{1,5},{5,9},{6,10},{7,11},{28,16... | collective-permute-start | bytes 786440 | tf_op jit(solution)/shard_map/ppermute | solution.py:444
  101.6 2.6 %collective-permute-start.1 = (bf16[128,1024]{1,0:T(8,128)(2,1)}, bf16[128,1024]{1,0:T(8,128)(2,1)}, u32[]{:S(2)}, u32[]{:S(2)}) collective-permute-start(bf16[128,1024]{1,0:T(8,128)(2,1)} %keys_values.1.refs_0_), channel_id=1, source_target_pairs={{14,0},{15,1},{0,2},{1,3},{2,4},{3,5},{5,7},{6,8},{7,9},{8,10},{9,... | collective-permute-start | bytes 786440 | tf_op jit(solution)/shard_map/ppermute | solution.py:444
  105.8 6.5 %all-to-all-start.2 = ((bf16[32,16,768]{2,1,0:T(8,128)(2,1)}), bf16[32,16,768]{2,1,0:T(8,128)(2,1)S(1)}, u32[]{:S(2)}, u32[]{:S(2)}) async-start(bf16[32,16,768]{2,1,0:T(8,128)(2,1)} %copy-done.2), calls=%async_computation.2 | async-start | bytes 1572864 | tf_op jit(solution)/shard_map/all_to_all | solution.py:490
  112.3 2.2 %collective-permute-start.5 = (bf16[128,1024]{1,0:T(8,128)(2,1)}, bf16[128,1024]{1,0:T(8,128)(2,1)S(1)}, u32[]{:S(2)}, u32[]{:S(2)}) collective-permute-start(bf16[128,1024]{1,0:T(8,128)(2,1)} %keys_values.1.refs_0_), channel_id=1, source_target_pairs={{0,1},{2,3},{6,7},{8,9},{10,11},{12,13},{14,15},{16,17},{18,19},{2... | collective-permute-start | bytes 786440 | tf_op jit(solution)/shard_map/ppermute | solution.py:446
  114.5 1.2 copy-done.1
  115.7 1.0 copy-done.3
  117.7 2.0 %collective-permute-done.2.refs_4_ = bf16[128,1024]{1,0:T(8,128)(2,1)} collective-permute-done((bf16[128,1024]{1,0:T(8,128)(2,1)}, bf16[128,1024]{1,0:T(8,128)(2,1)}, u32[]{:S(2)}, u32[]{:S(2)}) %collective-permute-start.2) | collective-permute-done | bytes 262176 | tf_op jit(solution)/shard_map/ppermute | solution.py:444
  119.7 2.8 %collective-permute-done.1.refs_2_ = bf16[128,1024]{1,0:T(8,128)(2,1)} collective-permute-done((bf16[128,1024]{1,0:T(8,128)(2,1)}, bf16[128,1024]{1,0:T(8,128)(2,1)}, u32[]{:S(2)}, u32[]{:S(2)}) %collective-permute-start.1) | collective-permute-done | bytes 262176 | tf_op jit(solution)/shard_map/ppermute | solution.py:444
  122.5 1.9 %collective-permute-start.6 = (bf16[128,1024]{1,0:T(8,128)(2,1)}, bf16[128,1024]{1,0:T(8,128)(2,1)S(1)}, u32[]{:S(2)}, u32[]{:S(2)}) collective-permute-start(bf16[128,1024]{1,0:T(8,128)(2,1)} %collective-permute-done.1.refs_2_), channel_id=1, source_target_pairs={{0,1},{1,0},{2,3},{3,2},{5,4},{7,6},{8,9},{9,8},{10,11},{11,10},{1... | collective-permute-start | bytes 786440 | tf_op jit(solution)/shard_map/ppermute | solution.py:446
  124.4 2.4 %collective-permute-start.7 = (bf16[128,1024]{1,0:T(8,128)(2,1)}, bf16[128,1024]{1,0:T(8,128)(2,1)S(1)}, u32[]{:S(2)}, u32[]{:S(2)}) collective-permute-start(bf16[128,1024]{1,0:T(8,128)(2,1)} %collective-permute-done.2.refs_4_), channel_id=1, source_target_pairs={{0,1},{1,0},{2,3},{3,2},{5,4},{9,8},{10,11},{11,10},{16,17},{17,16... | collective-permute-start | bytes 786440 | tf_op jit(solution)/shard_map/ppermute | solution.py:446
  128.3 5.8 %attend.1 = (bf16[128,2048]{1,0:T(8,128)(2,1)}, bf16[128,2048]{1,0:T(8,128)(2,1)S(1)}) custom-call(s32[1,128]{1,0:T(1,128)S(1)} %copy-done.7, bf16[4,512,128]{2,1,0:T(8,128)(2,1)S(1)} %queries.1, bf16[128,1024]{1,0:T(8,128)(2,1)} %keys_values.1.refs_0_, bf16[128,1024]{1,0:T(8,128)(2,1)S(1)} %collective-permute-done.5.refs_1_, ...), custom_call_target="tpu_custom_call" | custom-call | flops 12000000000 | bytes 8388608 | tf_op jit(solution)/shard_map/attend/pallas_call | solution.py:339
  134.0 3.3 %all-to-all-done.2 = bf16[32,16,768]{2,1,0:T(8,128)(2,1)S(1)} async-done(((bf16[32,16,768]{2,1,0:T(8,128)(2,1)}), bf16[32,16,768]{2,1,0:T(8,128)(2,1)S(1)}, u32[]{:S(2)}, u32[]{:S(2)}) %all-to-all-start.2) | async-done | bytes 786464 | tf_op jit(solution)/shard_map/all_to_all | solution.py:490
  137.3 1.8 %output.1 = bf16[128,4096]{1,0:T(8,128)(2,1)} custom-call(bf16[128,2048]{1,0:T(8,128)(2,1)S(1)} %get-tuple-element.22.attended_ref, bf16[2,16,16,768]{3,2,1,0:T(8,128)(2,1)S(1)} %bitcast.15), custom_call_target="tpu_custom_call" | custom-call | flops 100000000 | bytes 3145728 | tf_op jit(solution)/shard_map/output/pallas_call | solution.py:396
  (37 shorter events, 7.0 us)
Async XLA Ops:
  3.1 7.4 %copy-start.8 = (s32[3]{0:T(128)S(1)}, s32[3]{0:T(128)}, u32[]{:S(2)}) copy-start(s32[3]{0:T(128)} %param.14) | copy-start | bytes 40
  3.1 7.4 %copy-start.9 = (s32[3]{0:T(128)S(1)}, s32[3]{0:T(128)}, u32[]{:S(2)}) copy-start(s32[3]{0:T(128)} %param.13) | copy-start | bytes 40
  3.1 36.0 %all-to-all-start = ((bf16[16,16,2688]{2,1,0:T(8,128)(2,1)}), bf16[16,16,2688]{2,1,0:T(8,128)(2,1)S(1)}, u32[]{:S(2)}, u32[]{:S(2)}) async-start(bf16[16,16,2688]{2,1,0:T(8,128)(2,1)} %bitcast.16), calls=%async_computation | async-start | bytes 2752512 | tf_op jit(solution)/shard_map/all_to_all | solution.py:477
  10.5 3.6 %collective-permute-start = (s32[2,1,3]{2,0,1:T(2,128)S(1)}, s32[2,1,3]{2,0,1:T(2,128)S(1)}, u32[]{:S(2)}, u32[]{:S(2)}) collective-permute-start(s32[2,1,3]{2,0,1:T(2,128)S(1)} %add_bitcast_fusion), channel_id=1, source_target_pairs={{0,16},{16,0},{1,17},{17,1},{2,18},{18,2},{3,19},{19,3},{4,20},{20... | collective-permute-start | bytes 80 | tf_op jit(solution)/shard_map/ppermute | solution.py:481
  39.1 0.6 copy-start.6
  40.5 54.9 %copy-start = (bf16[128,4096]{1,0:T(8,128)(2,1)S(1)}, bf16[128,4096]{1,0:T(8,128)(2,1)}, u32[]{:S(2)}) copy-start(bf16[128,4096]{1,0:T(8,128)(2,1)} %hidden_ref.3) | copy-start | bytes 3145732
  40.5 54.9 %copy-start.4 = (bf16[128,512]{1,0:T(8,128)(2,1)S(1)}, bf16[128,512]{1,0:T(8,128)(2,1)}, u32[]{:S(2)}) copy-start(bf16[128,512]{1,0:T(8,128)(2,1)} %key_ref.1) | copy-start | bytes 393220
  40.5 54.9 %copy-start.5 = (bf16[128,512]{1,0:T(8,128)(2,1)S(1)}, bf16[128,512]{1,0:T(8,128)(2,1)}, u32[]{:S(2)}) copy-start(bf16[128,512]{1,0:T(8,128)(2,1)} %value_ref.1) | copy-start | bytes 393220
  95.3 8.8 %copy-start.7 = (s32[1,128]{1,0:T(1,128)S(1)}, s32[1,128]{1,0:T(1,128)}, u32[]{:S(2)}) copy-start(s32[1,128]{1,0:T(1,128)} %plan.1.plan_ref) | copy-start | bytes 1540
  96.8 20.9 %collective-permute-start.4 = (bf16[128,1024]{1,0:T(8,128)(2,1)}, bf16[128,1024]{1,0:T(8,128)(2,1)}, u32[]{:S(2)}, u32[]{:S(2)}) collective-permute-start(bf16[128,1024]{1,0:T(8,128)(2,1)} %keys_values.1.refs_0_), channel_id=1, source_target_pairs={{12,4},{13,5},{28,20},{29,21}} | collective-permute-start | bytes 786440 | tf_op jit(solution)/shard_map/ppermute | solution.py:444
  98.2 19.6 %collective-permute-start.3 = (bf16[128,1024]{1,0:T(8,128)(2,1)}, bf16[128,1024]{1,0:T(8,128)(2,1)}, u32[]{:S(2)}, u32[]{:S(2)}) collective-permute-start(bf16[128,1024]{1,0:T(8,128)(2,1)} %keys_values.1.refs_0_), channel_id=1, source_target_pairs={{12,2},{13,3},{14,4},{15,5},{5,11},{28,18},{29,19},{30,20},{31,21}... | collective-permute-start | bytes 786440 | tf_op jit(solution)/shard_map/ppermute | solution.py:444
  99.5 20.2 %collective-permute-start.2 = (bf16[128,1024]{1,0:T(8,128)(2,1)}, bf16[128,1024]{1,0:T(8,128)(2,1)}, u32[]{:S(2)}, u32[]{:S(2)}) collective-permute-start(bf16[128,1024]{1,0:T(8,128)(2,1)} %keys_values.1.refs_0_), channel_id=1, source_target_pairs={{12,0},{13,1},{14,2},{15,3},{0,4},{1,5},{5,9},{6,10},{7,11},{28,16... | collective-permute-start | bytes 786440 | tf_op jit(solution)/shard_map/ppermute | solution.py:444
  101.6 20.9 %collective-permute-start.1 = (bf16[128,1024]{1,0:T(8,128)(2,1)}, bf16[128,1024]{1,0:T(8,128)(2,1)}, u32[]{:S(2)}, u32[]{:S(2)}) collective-permute-start(bf16[128,1024]{1,0:T(8,128)(2,1)} %keys_values.1.refs_0_), channel_id=1, source_target_pairs={{14,0},{15,1},{0,2},{1,3},{2,4},{3,5},{5,7},{6,8},{7,9},{8,10},{9,... | collective-permute-start | bytes 786440 | tf_op jit(solution)/shard_map/ppermute | solution.py:444
  104.9 0.9 copy-start.2
  105.8 31.6 %all-to-all-start.2 = ((bf16[32,16,768]{2,1,0:T(8,128)(2,1)}), bf16[32,16,768]{2,1,0:T(8,128)(2,1)S(1)}, u32[]{:S(2)}, u32[]{:S(2)}) async-start(bf16[32,16,768]{2,1,0:T(8,128)(2,1)} %copy-done.2), calls=%async_computation.2 | async-start | bytes 1572864 | tf_op jit(solution)/shard_map/all_to_all | solution.py:490
  112.3 15.9 %collective-permute-start.5 = (bf16[128,1024]{1,0:T(8,128)(2,1)}, bf16[128,1024]{1,0:T(8,128)(2,1)S(1)}, u32[]{:S(2)}, u32[]{:S(2)}) collective-permute-start(bf16[128,1024]{1,0:T(8,128)(2,1)} %keys_values.1.refs_0_), channel_id=1, source_target_pairs={{0,1},{2,3},{6,7},{8,9},{10,11},{12,13},{14,15},{16,17},{18,19},{2... | collective-permute-start | bytes 786440 | tf_op jit(solution)/shard_map/ppermute | solution.py:446
  114.5 1.2 copy-start.1
  115.7 1.0 copy-start.3
  122.5 5.7 %collective-permute-start.6 = (bf16[128,1024]{1,0:T(8,128)(2,1)}, bf16[128,1024]{1,0:T(8,128)(2,1)S(1)}, u32[]{:S(2)}, u32[]{:S(2)}) collective-permute-start(bf16[128,1024]{1,0:T(8,128)(2,1)} %collective-permute-done.1.refs_2_), channel_id=1, source_target_pairs={{0,1},{1,0},{2,3},{3,2},{5,4},{7,6},{8,9},{9,8},{10,11},{11,10},{1... | collective-permute-start | bytes 786440 | tf_op jit(solution)/shard_map/ppermute | solution.py:446
  124.4 3.8 %collective-permute-start.7 = (bf16[128,1024]{1,0:T(8,128)(2,1)}, bf16[128,1024]{1,0:T(8,128)(2,1)S(1)}, u32[]{:S(2)}, u32[]{:S(2)}) collective-permute-start(bf16[128,1024]{1,0:T(8,128)(2,1)} %collective-permute-done.2.refs_4_), channel_id=1, source_target_pairs={{0,1},{1,0},{2,3},{3,2},{5,4},{9,8},{10,11},{11,10},{16,17},{17,16... | collective-permute-start | bytes 786440 | tf_op jit(solution)/shard_map/ppermute | solution.py:446
  126.8 1.4 %collective-permute-start.8 = (bf16[128,1024]{1,0:T(8,128)(2,1)}, bf16[128,1024]{1,0:T(8,128)(2,1)S(1)}, u32[]{:S(2)}, u32[]{:S(2)}) collective-permute-start(bf16[128,1024]{1,0:T(8,128)(2,1)} %collective-permute-done.3.refs_6_), channel_id=1, source_target_pairs={{2,3},{3,2},{5,4},{11,10},{18,19},{19,18},{21,20},{27,26}} | collective-permute-start | bytes 786440 | tf_op jit(solution)/shard_map/ppermute | solution.py:446
  127.5 0.7 collective-permute-start.9

commit v3 on v2

--- a/solution.py
+++ b/solution.py
@@ -439,9 +439,21 @@
     return [(d, d ^ 1) for d in range(shards) if (d - shift) % shards in earlier[d ^ 1]]
 
 
-def exchange(kv, queries, shards, reach):
+DETOUR_SHIFT, DETOUR_FIRST, DETOUR_VIA = 6, (4, 5), 2
+
+
+def exchange(kv, queries, shards, reach, detour):
     shifts = range(0, reach + 1, 2)
-    got = [kv] + [lax.ppermute(kv, "ctx", shift_pairs(shards, s)) for s in shifts[1:]]
+    routes = [shift_pairs(shards, s) for s in shifts]
+    if detour:
+        direct, later = DETOUR_SHIFT // 2, (DETOUR_SHIFT + DETOUR_VIA) // 2
+        turned = [(s, d) for s, d in routes[direct] if d in DETOUR_FIRST]
+        routes[direct] = [pair for pair in routes[direct] if pair not in turned]
+        routes[later] = routes[later] + [(s, d + DETOUR_VIA) for s, d in turned]
+    got = [kv] + [lax.ppermute(kv, "ctx", route) for route in routes[1:]]
+    if detour:
+        hop = lax.ppermute(got[later], "ctx", [(d + DETOUR_VIA, d) for _, d in turned])
+        got[direct] = got[direct] + hop
     got[1:], queries = lax.optimization_barrier((got[1:], queries))
     swapped = [lax.ppermute(b, "ctx", swap_pairs(shards, s)) for s, b in zip(shifts, got)]
     blocks, steps = [kv], [(0, True)]
@@ -481,9 +493,10 @@
         theirs = lax.ppermute(requests, "groups", [(0, 1), (1, 0)])
         requests = jnp.concatenate([requests, theirs], axis=1)
     plan = make_plan(shards, reach, me, requests[0], requests[1], adapter_owner)
+    plan = jnp.maximum(plan, 0)
     positions = (plan[0, COUNT] - 1) * tokens + jnp.arange(tokens, dtype=jnp.int32)
     tables = rope_tables(positions)
-    spread, tables = lax.optimization_barrier((spread, tables))
+    spread, tables, plan = lax.optimization_barrier((spread, tables, plan))
 
     def collect(pieces):
         axes = ("groups", "ctx") if halves == 2 else "ctx"
@@ -495,7 +508,7 @@
     pieces = collect(route(plan, spread, dests, 0, kv_width + q_width))
     kv = make_keys_values(hidden, frozen_key, frozen_value, tables, pieces)
     queries = make_queries(hidden, frozen_query, tables, pieces, kv_width)
-    blocks, steps, queries = exchange(kv, queries, shards, reach)
+    blocks, steps, queries = exchange(kv, queries, shards, reach, halves == 2)
     later = route(plan, spread, dests, kv_width + q_width, o_width)
     kv, later = lax.optimization_barrier((kv, later))
     later = collect(later)

time: 140 us -> 147 us (1.050)
  starting transfers between devices: 30.6 us -> 40.6 us
  waiting for transfers between devices: 30.2 us -> 25.6 us
  other arithmetic: 1.67 us -> 3.3 us
    ppermute x4 -> x5, starting transfers between devices: 7.33 us -> 17.7 us  [the longest x4 16.4 us: exchange(): got = [kv] + [lax.ppermute(kv, 'ctx', route) for route in routes[1:]]]
    ppermute x4 -> x5, waiting for transfers between devices: 4.8 us -> 0.01 us  [the longest x4 0.01 us: exchange(): got = [kv] + [lax.ppermute(kv, 'ctx', route) for route in routes[1:]]]
    unnamed x20 -> x16, local copies, waits for them, and re-layouts: 3.78 us -> 3.17 us
  transfers between devices with their start and end apart: 12 -> 13, of which waited for: 5 -> 3; matrix products, arithmetic and copies ran while one was open for 2% -> 3% of each run, Pallas kernels for 6% -> 6%
where the time goes in v3:
time: 147 us; the launch traced here: 146 us
  blocking collectives  54.8 us (37%)
  starting transfers between devices  40.6 us (28%)
  waiting for transfers between devices  25.6 us (17%)
  Pallas kernels  16.2 us (11%)
  local copies, waits for them, and re-layouts  3.75 us (3%)
  other arithmetic  3.3 us (2%)
  between operations  1.57 us (1%)
    all_to_all x1, blocking collectives, collect(): lax.all_to_all(pieces, axes, split_axis=0, concat_axis=0, tiled=True)  54.8 us
    all_to_all x1, waiting for transfers between devices, body(): lax.all_to_all(packed, 'ctx', split_axis=0, concat_axis=0, tiled=True)  20.7 us
    ppermute x4, starting transfers between devices, exchange(): got = [kv] + [lax.ppermute(kv, 'ctx', route) for route in routes[1:]]  16.4 us
    ppermute x5, starting transfers between devices, exchange(): lax.ppermute(b, 'ctx', swap_pairs(shards, s))  7.79 us
    all_to_all x1, starting transfers between devices, body(): lax.all_to_all(packed, 'ctx', split_axis=0, concat_axis=0, tiled=True)  7.4 us
    all_to_all x1, starting transfers between devices, collect(): lax.all_to_all(pieces, axes, split_axis=0, concat_axis=0, tiled=True)  6.11 us
    pallas_call x1, Pallas kernels, attend(): pl.pallas_call(functools.partial(attend_kernel, steps), out_shape=[jax.Sh...  5.8 us
    all_to_all x1, waiting for transfers between devices, collect(): lax.all_to_all(pieces, axes, split_axis=0, concat_axis=0, tiled=True)  3.44 us
  transfers between devices with their start and end apart: 13, of which 3 were waited for; matrix products, arithmetic and copies ran while one was open for 3% of the time, Pallas kernels for 6%

profile of v3, /device:TPU:0, one launch (start us, length us, event | category | flops | bytes accessed | tf_op | source)
XLA Modules:
  0.0 145.9 jit_solution(40775949643387929)
XLA Ops:
  0.6 2.5 %pack.1 = bf16[1,4,4,16,2688]{4,3,2,1,0:T(8,128)(2,1)} custom-call(bf16[4,16,21504]{2,1,0:T(8,128)(2,1)} %bitcast.16), custom_call_target="tpu_custom_call" | custom-call | tf_op jit(solution)/shard_map/pack/pallas_call | solution.py:137
  3.1 7.4 %all-to-all-start = ((bf16[16,16,2688]{2,1,0:T(8,128)(2,1)}), bf16[16,16,2688]{2,1,0:T(8,128)(2,1)S(1)}, u32[]{:S(2)}, u32[]{:S(2)}) async-start(bf16[16,16,2688]{2,1,0:T(8,128)(2,1)} %bitcast.15), calls=%async_computation | async-start | bytes 2752512 | tf_op jit(solution)/shard_map/all_to_all | solution.py:489
  10.6 1.6 %collective-permute-start = (s32[2,1,3]{2,0,1:T(2,128)S(1)}, s32[2,1,3]{2,0,1:T(2,128)S(1)}, u32[]{:S(2)}, u32[]{:S(2)}) collective-permute-start(s32[2,1,3]{2,0,1:T(2,128)S(1)} %add_bitcast_fusion), channel_id=1, source_target_pairs={{0,16},{16,0},{1,17},{17,1},{2,18},{18,2},{3,19},{19,3},{4,20},{20... | collective-permute-start | bytes 80 | tf_op jit(solution)/shard_map/ppermute | solution.py:493
  12.7 1.5 %collective-permute-done = s32[2,1,3]{2,0,1:T(2,128)S(1)} collective-permute-done((s32[2,1,3]{2,0,1:T(2,128)S(1)}, s32[2,1,3]{2,0,1:T(2,128)S(1)}, u32[]{:S(2)}, u32[]{:S(2)}) %collective-permute-start) | collective-permute-done | bytes 56 | tf_op jit(solution)/shard_map/ppermute | solution.py:493
  14.8 1.4 plan.1
  18.4 20.7 %all-to-all-done.spread_ref = bf16[16,16,2688]{2,1,0:T(8,128)(2,1)S(1)} async-done(((bf16[16,16,2688]{2,1,0:T(8,128)(2,1)}), bf16[16,16,2688]{2,1,0:T(8,128)(2,1)S(1)}, u32[]{:S(2)}, u32[]{:S(2)}) %all-to-all-start) | async-done | bytes 1376288 | tf_op jit(solution)/shard_map/all_to_all | solution.py:489
  39.9 54.8 %all_to_all.15 = bf16[32,16,1920]{2,1,0:T(8,128)(2,1)S(1)} all-to-all(bf16[32,16,1920]{2,1,0:T(8,128)(2,1)S(1)} %route.2), channel_id=1, replica_groups=mesh['groups'=2,'ctx'=16] {'groups','ctx'}, dimensions={0} | all-to-all | bytes 3932160 | tf_op jit(solution)/shard_map/all_to_all | solution.py:503
  94.7 1.5 %keys_values.1.refs_0_ = bf16[128,1024]{1,0:T(8,128)(2,1)} custom-call(bf16[128,4096]{1,0:T(8,128)(2,1)S(1)} %copy-done, bf16[128,512]{1,0:T(8,128)(2,1)S(1)} %copy-done.4, bf16[128,512]{1,0:T(8,128)(2,1)S(1)} %copy-done.5, f32[128,128]{1,0:T(8,128)S(1)} %get-tuple-element.15.cos_ref, f32[128,128]{1,0:T(8,128)S(1)} %get-tuple-element.16.sin_ref, ...), custom_call_target="tpu_custom_call" | custom-call | flops 150000000 | bytes 3145728 | tf_op jit(solution)/shard_map/keys_values/pallas_call | solution.py:219
  96.2 1.4 collective-permute-start.4
  97.6 1.4 collective-permute-start.3
  98.9 1.4 collective-permute-start.5
  100.3 11.7 %collective-permute-start.2 = (bf16[128,1024]{1,0:T(8,128)(2,1)}, bf16[128,1024]{1,0:T(8,128)(2,1)}, u32[]{:S(2)}, u32[]{:S(2)}) collective-permute-start(bf16[128,1024]{1,0:T(8,128)(2,1)} %keys_values.1.refs_0_), channel_id=1, source_target_pairs={{12,0},{13,1},{14,2},{15,3},{0,4},{1,5},{5,9},{6,10},{7,11},{28,16... | collective-permute-start | bytes 786440 | tf_op jit(solution)/shard_map/ppermute | solution.py:453
  112.0 1.9 %collective-permute-start.1 = (bf16[128,1024]{1,0:T(8,128)(2,1)}, bf16[128,1024]{1,0:T(8,128)(2,1)}, u32[]{:S(2)}, u32[]{:S(2)}) collective-permute-start(bf16[128,1024]{1,0:T(8,128)(2,1)} %keys_values.1.refs_0_), channel_id=1, source_target_pairs={{14,0},{15,1},{0,2},{1,3},{2,4},{3,5},{5,7},{6,8},{7,9},{8,10},{9,... | collective-permute-start | bytes 786440 | tf_op jit(solution)/shard_map/ppermute | solution.py:453
  115.5 6.1 %all-to-all-start.2 = ((bf16[32,16,768]{2,1,0:T(8,128)(2,1)}), bf16[32,16,768]{2,1,0:T(8,128)(2,1)}, u32[]{:S(2)}, u32[]{:S(2)}) async-start(bf16[32,16,768]{2,1,0:T(8,128)(2,1)} %copy-done.2), calls=%async_computation.2 | async-start | bytes 1572864 | tf_op jit(solution)/shard_map/all_to_all | solution.py:503
  121.7 2.1 %collective-permute-start.6 = (bf16[128,1024]{1,0:T(8,128)(2,1)}, bf16[128,1024]{1,0:T(8,128)(2,1)S(1)}, u32[]{:S(2)}, u32[]{:S(2)}) collective-permute-start(bf16[128,1024]{1,0:T(8,128)(2,1)} %keys_values.1.refs_0_), channel_id=1, source_target_pairs={{0,1},{2,3},{6,7},{8,9},{10,11},{12,13},{14,15},{16,17},{18,19},{2... | collective-permute-start | bytes 786440 | tf_op jit(solution)/shard_map/ppermute | solution.py:458
  123.8 1.2 copy-done.1
  125.0 1.0 copy-done.3
  126.0 1.0 queries.1
  127.0 1.1 add.17.refs_6_
  128.2 1.9 %collective-permute-start.7 = (bf16[128,1024]{1,0:T(8,128)(2,1)}, bf16[128,1024]{1,0:T(8,128)(2,1)S(1)}, u32[]{:S(2)}, u32[]{:S(2)}) collective-permute-start(bf16[128,1024]{1,0:T(8,128)(2,1)} %collective-permute-done.1.refs_2_), channel_id=1, source_target_pairs={{0,1},{1,0},{2,3},{3,2},{5,4},{7,6},{8,9},{9,8},{10,11},{11,10},{1... | collective-permute-start | bytes 786440 | tf_op jit(solution)/shard_map/ppermute | solution.py:458
  130.1 2.4 %collective-permute-start.8 = (bf16[128,1024]{1,0:T(8,128)(2,1)}, bf16[128,1024]{1,0:T(8,128)(2,1)S(1)}, u32[]{:S(2)}, u32[]{:S(2)}) collective-permute-start(bf16[128,1024]{1,0:T(8,128)(2,1)} %collective-permute-done.2.refs_4_), channel_id=1, source_target_pairs={{0,1},{1,0},{2,3},{3,2},{5,4},{9,8},{10,11},{11,10},{16,17},{17,16... | collective-permute-start | bytes 786440 | tf_op jit(solution)/shard_map/ppermute | solution.py:458
  133.9 5.8 %attend.1 = (bf16[128,2048]{1,0:T(8,128)(2,1)}, bf16[128,2048]{1,0:T(8,128)(2,1)S(1)}) custom-call(s32[1,128]{1,0:T(1,128)S(1)} %broadcast_maximum_fusion.plan_ref, bf16[4,512,128]{2,1,0:T(8,128)(2,1)S(1)} %queries.1, bf16[128,1024]{1,0:T(8,128)(2,1)} %keys_values.1.refs_0_, bf16[128,1024]{1,0:T(8,128)(2,1)S(1)} %collective-permute-done.6.refs_1_, ...), custom_call_target="tpu_custom_call" | custom-call | flops 12000000000 | bytes 8388608 | tf_op jit(solution)/shard_map/attend/pallas_call | solution.py:339
  139.7 3.4 %all-to-all-done.2 = bf16[32,16,768]{2,1,0:T(8,128)(2,1)} async-done(((bf16[32,16,768]{2,1,0:T(8,128)(2,1)}), bf16[32,16,768]{2,1,0:T(8,128)(2,1)}, u32[]{:S(2)}, u32[]{:S(2)}) %all-to-all-start.2) | async-done | bytes 786464 | tf_op jit(solution)/shard_map/all_to_all | solution.py:503
  143.2 2.7 %output.1 = bf16[128,4096]{1,0:T(8,128)(2,1)} custom-call(bf16[128,2048]{1,0:T(8,128)(2,1)S(1)} %get-tuple-element.24.attended_ref, bf16[2,16,16,768]{3,2,1,0:T(8,128)(2,1)} %bitcast.11.piece_ref), custom_call_target="tpu_custom_call" | custom-call | flops 100000000 | bytes 3145728 | tf_op jit(solution)/shard_map/output/pallas_call | solution.py:396
  (37 shorter events, 6.6 us)
Async XLA Ops:
  3.1 7.4 %copy-start.6 = (s32[3]{0:T(128)S(1)}, s32[3]{0:T(128)}, u32[]{:S(2)}) copy-start(s32[3]{0:T(128)} %param.14) | copy-start | bytes 40
  3.1 7.4 %copy-start.7 = (s32[3]{0:T(128)S(1)}, s32[3]{0:T(128)}, u32[]{:S(2)}) copy-start(s32[3]{0:T(128)} %param.13) | copy-start | bytes 40
  3.1 36.0 %all-to-all-start = ((bf16[16,16,2688]{2,1,0:T(8,128)(2,1)}), bf16[16,16,2688]{2,1,0:T(8,128)(2,1)S(1)}, u32[]{:S(2)}, u32[]{:S(2)}) async-start(bf16[16,16,2688]{2,1,0:T(8,128)(2,1)} %bitcast.15), calls=%async_computation | async-start | bytes 2752512 | tf_op jit(solution)/shard_map/all_to_all | solution.py:489
  10.6 3.6 %collective-permute-start = (s32[2,1,3]{2,0,1:T(2,128)S(1)}, s32[2,1,3]{2,0,1:T(2,128)S(1)}, u32[]{:S(2)}, u32[]{:S(2)}) collective-permute-start(s32[2,1,3]{2,0,1:T(2,128)S(1)} %add_bitcast_fusion), channel_id=1, source_target_pairs={{0,16},{16,0},{1,17},{17,1},{2,18},{18,2},{3,19},{19,3},{4,20},{20... | collective-permute-start | bytes 80 | tf_op jit(solution)/shard_map/ppermute | solution.py:493
  39.9 54.9 %copy-start = (bf16[128,4096]{1,0:T(8,128)(2,1)S(1)}, bf16[128,4096]{1,0:T(8,128)(2,1)}, u32[]{:S(2)}) copy-start(bf16[128,4096]{1,0:T(8,128)(2,1)} %hidden_ref.3) | copy-start | bytes 3145732
  39.9 54.9 %copy-start.4 = (bf16[128,512]{1,0:T(8,128)(2,1)S(1)}, bf16[128,512]{1,0:T(8,128)(2,1)}, u32[]{:S(2)}) copy-start(bf16[128,512]{1,0:T(8,128)(2,1)} %key_ref.1) | copy-start | bytes 393220
  39.9 54.9 %copy-start.5 = (bf16[128,512]{1,0:T(8,128)(2,1)S(1)}, bf16[128,512]{1,0:T(8,128)(2,1)}, u32[]{:S(2)}) copy-start(bf16[128,512]{1,0:T(8,128)(2,1)} %value_ref.1) | copy-start | bytes 393220
  96.2 2.7 %collective-permute-start.4 = (bf16[128,1024]{1,0:T(8,128)(2,1)}, bf16[128,1024]{1,0:T(8,128)(2,1)}, u32[]{:S(2)}, u32[]{:S(2)}) collective-permute-start(bf16[128,1024]{1,0:T(8,128)(2,1)} %keys_values.1.refs_0_), channel_id=1, source_target_pairs={{12,4},{13,5},{14,6},{15,7},{28,20},{29,21},{30,22},{31,23}} | collective-permute-start | bytes 786440 | tf_op jit(solution)/shard_map/ppermute | solution.py:453
  97.6 29.5 %collective-permute-start.3 = (bf16[128,1024]{1,0:T(8,128)(2,1)}, bf16[128,1024]{1,0:T(8,128)(2,1)}, u32[]{:S(2)}, u32[]{:S(2)}) collective-permute-start(bf16[128,1024]{1,0:T(8,128)(2,1)} %keys_values.1.refs_0_), channel_id=1, source_target_pairs={{12,2},{13,3},{5,11},{28,18},{29,19},{21,27}} | collective-permute-start | bytes 786440 | tf_op jit(solution)/shard_map/ppermute | solution.py:453
  98.9 28.1 %collective-permute-start.5 = (bf16[128,1024]{1,0:T(8,128)(2,1)}, bf16[128,1024]{1,0:T(8,128)(2,1)}, u32[]{:S(2)}, u32[]{:S(2)}) collective-permute-start(bf16[128,1024]{1,0:T(8,128)(2,1)} %collective-permute-done.4.refs_8_), channel_id=1, source_target_pairs={{6,4},{7,5},{22,20},{23,21}} | collective-permute-start | bytes 786440 | tf_op jit(solution)/shard_map/ppermute | solution.py:455
  100.3 27.8 %collective-permute-start.2 = (bf16[128,1024]{1,0:T(8,128)(2,1)}, bf16[128,1024]{1,0:T(8,128)(2,1)}, u32[]{:S(2)}, u32[]{:S(2)}) collective-permute-start(bf16[128,1024]{1,0:T(8,128)(2,1)} %keys_values.1.refs_0_), channel_id=1, source_target_pairs={{12,0},{13,1},{14,2},{15,3},{0,4},{1,5},{5,9},{6,10},{7,11},{28,16... | collective-permute-start | bytes 786440 | tf_op jit(solution)/shard_map/ppermute | solution.py:453
  112.0 16.1 %collective-permute-start.1 = (bf16[128,1024]{1,0:T(8,128)(2,1)}, bf16[128,1024]{1,0:T(8,128)(2,1)}, u32[]{:S(2)}, u32[]{:S(2)}) collective-permute-start(bf16[128,1024]{1,0:T(8,128)(2,1)} %keys_values.1.refs_0_), channel_id=1, source_target_pairs={{14,0},{15,1},{0,2},{1,3},{2,4},{3,5},{5,7},{6,8},{7,9},{8,10},{9,... | collective-permute-start | bytes 786440 | tf_op jit(solution)/shard_map/ppermute | solution.py:453
  114.7 0.9 copy-start.2
  115.5 27.6 %all-to-all-start.2 = ((bf16[32,16,768]{2,1,0:T(8,128)(2,1)}), bf16[32,16,768]{2,1,0:T(8,128)(2,1)}, u32[]{:S(2)}, u32[]{:S(2)}) async-start(bf16[32,16,768]{2,1,0:T(8,128)(2,1)} %copy-done.2), calls=%async_computation.2 | async-start | bytes 1572864 | tf_op jit(solution)/shard_map/all_to_all | solution.py:503
  121.7 12.2 %collective-permute-start.6 = (bf16[128,1024]{1,0:T(8,128)(2,1)}, bf16[128,1024]{1,0:T(8,128)(2,1)S(1)}, u32[]{:S(2)}, u32[]{:S(2)}) collective-permute-start(bf16[128,1024]{1,0:T(8,128)(2,1)} %keys_values.1.refs_0_), channel_id=1, source_target_pairs={{0,1},{2,3},{6,7},{8,9},{10,11},{12,13},{14,15},{16,17},{18,19},{2... | collective-permute-start | bytes 786440 | tf_op jit(solution)/shard_map/ppermute | solution.py:458
  123.8 1.2 copy-start.1
  125.0 1.0 copy-start.3
  128.2 5.7 %collective-permute-start.7 = (bf16[128,1024]{1,0:T(8,128)(2,1)}, bf16[128,1024]{1,0:T(8,128)(2,1)S(1)}, u32[]{:S(2)}, u32[]{:S(2)}) collective-permute-start(bf16[128,1024]{1,0:T(8,128)(2,1)} %collective-permute-done.1.refs_2_), channel_id=1, source_target_pairs={{0,1},{1,0},{2,3},{3,2},{5,4},{7,6},{8,9},{9,8},{10,11},{11,10},{1... | collective-permute-start | bytes 786440 | tf_op jit(solution)/shard_map/ppermute | solution.py:458
  130.1 3.8 %collective-permute-start.8 = (bf16[128,1024]{1,0:T(8,128)(2,1)}, bf16[128,1024]{1,0:T(8,128)(2,1)S(1)}, u32[]{:S(2)}, u32[]{:S(2)}) collective-permute-start(bf16[128,1024]{1,0:T(8,128)(2,1)} %collective-permute-done.2.refs_4_), channel_id=1, source_target_pairs={{0,1},{1,0},{2,3},{3,2},{5,4},{9,8},{10,11},{11,10},{16,17},{17,16... | collective-permute-start | bytes 786440 | tf_op jit(solution)/shard_map/ppermute | solution.py:458
  132.5 1.4 collective-permute-start.9
  133.2 0.7 collective-permute-start.10

commit v4 on v2

--- a/solution.py
+++ b/solution.py
@@ -481,9 +481,10 @@
         theirs = lax.ppermute(requests, "groups", [(0, 1), (1, 0)])
         requests = jnp.concatenate([requests, theirs], axis=1)
     plan = make_plan(shards, reach, me, requests[0], requests[1], adapter_owner)
+    plan = jnp.maximum(plan, 0)
     positions = (plan[0, COUNT] - 1) * tokens + jnp.arange(tokens, dtype=jnp.int32)
     tables = rope_tables(positions)
-    spread, tables = lax.optimization_barrier((spread, tables))
+    spread, tables, plan = lax.optimization_barrier((spread, tables, plan))
 
     def collect(pieces):
         axes = ("groups", "ctx") if halves == 2 else "ctx"

time: 140 us -> 139 us (level)
    unnamed x20 -> x16, local copies, waits for them, and re-layouts: 3.78 us -> 3.17 us
where the time goes in v4:
time: 139 us
  blocking collectives  54.8 us (39%)
  starting transfers between devices  30.6 us (22%)
  waiting for transfers between devices  30.2 us (22%)
  Pallas kernels  15.3 us (11%)
  local copies, waits for them, and re-layouts  3.75 us (3%)
  other arithmetic  2.28 us (2%)
  between operations  1.55 us (1%)
    all_to_all x1, blocking collectives, collect(): lax.all_to_all(pieces, axes, split_axis=0, concat_axis=0, tiled=True)  54.8 us
    all_to_all x1, waiting for transfers between devices, body(): lax.all_to_all(packed, 'ctx', split_axis=0, concat_axis=0, tiled=True)  20.7 us
    ppermute x5, starting transfers between devices, exchange(): lax.ppermute(b, 'ctx', swap_pairs(shards, s))  7.84 us
    all_to_all x1, starting transfers between devices, body(): lax.all_to_all(packed, 'ctx', split_axis=0, concat_axis=0, tiled=True)  7.4 us
    ppermute x4, starting transfers between devices, exchange(): lax.ppermute(kv, 'ctx', shift_pairs(shards, s))  7.33 us
    all_to_all x1, starting transfers between devices, collect(): lax.all_to_all(pieces, axes, split_axis=0, concat_axis=0, tiled=True)  6.5 us
    pallas_call x1, Pallas kernels, attend(): pl.pallas_call(functools.partial(attend_kernel, steps), out_shape=[jax.Sh...  5.77 us
    ppermute x4, waiting for transfers between devices, exchange(): lax.ppermute(kv, 'ctx', shift_pairs(shards, s))  4.79 us
  transfers between devices with their start and end apart: 12, of which 5 were waited for; matrix products, arithmetic and copies ran while one was open for 2% of the time, Pallas kernels for 6%

profile of v4, /device:TPU:0, one launch (start us, length us, event | category | flops | bytes accessed | tf_op | source)
XLA Modules:
  0.0 138.5 jit_solution(11669697696093033827)
XLA Ops:
  0.6 2.4 %pack.1 = bf16[1,4,4,16,2688]{4,3,2,1,0:T(8,128)(2,1)} custom-call(bf16[4,16,21504]{2,1,0:T(8,128)(2,1)} %bitcast.17), custom_call_target="tpu_custom_call" | custom-call | tf_op jit(solution)/shard_map/pack/pallas_call | solution.py:137
  3.1 7.4 %all-to-all-start = ((bf16[16,16,2688]{2,1,0:T(8,128)(2,1)}), bf16[16,16,2688]{2,1,0:T(8,128)(2,1)S(1)}, u32[]{:S(2)}, u32[]{:S(2)}) async-start(bf16[16,16,2688]{2,1,0:T(8,128)(2,1)} %bitcast.16), calls=%async_computation | async-start | bytes 2752512 | tf_op jit(solution)/shard_map/all_to_all | solution.py:477
  10.5 1.6 %collective-permute-start = (s32[2,1,3]{2,0,1:T(2,128)S(1)}, s32[2,1,3]{2,0,1:T(2,128)S(1)}, u32[]{:S(2)}, u32[]{:S(2)}) collective-permute-start(s32[2,1,3]{2,0,1:T(2,128)S(1)} %add_bitcast_fusion), channel_id=1, source_target_pairs={{0,16},{16,0},{1,17},{17,1},{2,18},{18,2},{3,19},{19,3},{4,20},{20... | collective-permute-start | bytes 80 | tf_op jit(solution)/shard_map/ppermute | solution.py:481
  12.8 1.4 %collective-permute-done = s32[2,1,3]{2,0,1:T(2,128)S(1)} collective-permute-done((s32[2,1,3]{2,0,1:T(2,128)S(1)}, s32[2,1,3]{2,0,1:T(2,128)S(1)}, u32[]{:S(2)}, u32[]{:S(2)}) %collective-permute-start) | collective-permute-done | bytes 56 | tf_op jit(solution)/shard_map/ppermute | solution.py:481
  14.7 1.4 plan.1
  18.4 20.7 %all-to-all-done.spread_ref = bf16[16,16,2688]{2,1,0:T(8,128)(2,1)S(1)} async-done(((bf16[16,16,2688]{2,1,0:T(8,128)(2,1)}), bf16[16,16,2688]{2,1,0:T(8,128)(2,1)S(1)}, u32[]{:S(2)}, u32[]{:S(2)}) %all-to-all-start) | async-done | bytes 1376288 | tf_op jit(solution)/shard_map/all_to_all | solution.py:477
  39.9 54.8 %all_to_all.15 = bf16[32,16,1920]{2,1,0:T(8,128)(2,1)S(1)} all-to-all(bf16[32,16,1920]{2,1,0:T(8,128)(2,1)S(1)} %route.2), channel_id=1, replica_groups=mesh['groups'=2,'ctx'=16] {'groups','ctx'}, dimensions={0} | all-to-all | bytes 3932160 | tf_op jit(solution)/shard_map/all_to_all | solution.py:491
  94.7 1.5 %keys_values.1.refs_0_ = bf16[128,1024]{1,0:T(8,128)(2,1)} custom-call(bf16[128,4096]{1,0:T(8,128)(2,1)S(1)} %copy-done, bf16[128,512]{1,0:T(8,128)(2,1)S(1)} %copy-done.4, bf16[128,512]{1,0:T(8,128)(2,1)S(1)} %copy-done.5, f32[128,128]{1,0:T(8,128)S(1)} %get-tuple-element.15.cos_ref, f32[128,128]{1,0:T(8,128)S(1)} %get-tuple-element.16.sin_ref, ...), custom_call_target="tpu_custom_call" | custom-call | flops 150000000 | bytes 3145728 | tf_op jit(solution)/shard_map/keys_values/pallas_call | solution.py:219
  96.2 1.4 collective-permute-start.4
  97.5 1.4 collective-permute-start.3
  98.9 2.0 %collective-permute-start.2 = (bf16[128,1024]{1,0:T(8,128)(2,1)}, bf16[128,1024]{1,0:T(8,128)(2,1)}, u32[]{:S(2)}, u32[]{:S(2)}) collective-permute-start(bf16[128,1024]{1,0:T(8,128)(2,1)} %keys_values.1.refs_0_), channel_id=1, source_target_pairs={{12,0},{13,1},{14,2},{15,3},{0,4},{1,5},{5,9},{6,10},{7,11},{28,16... | collective-permute-start | bytes 786440 | tf_op jit(solution)/shard_map/ppermute | solution.py:444
  101.0 2.6 %collective-permute-start.1 = (bf16[128,1024]{1,0:T(8,128)(2,1)}, bf16[128,1024]{1,0:T(8,128)(2,1)}, u32[]{:S(2)}, u32[]{:S(2)}) collective-permute-start(bf16[128,1024]{1,0:T(8,128)(2,1)} %keys_values.1.refs_0_), channel_id=1, source_target_pairs={{14,0},{15,1},{0,2},{1,3},{2,4},{3,5},{5,7},{6,8},{7,9},{8,10},{9,... | collective-permute-start | bytes 786440 | tf_op jit(solution)/shard_map/ppermute | solution.py:444
  105.1 6.5 %all-to-all-start.2 = ((bf16[32,16,768]{2,1,0:T(8,128)(2,1)}), bf16[32,16,768]{2,1,0:T(8,128)(2,1)S(1)}, u32[]{:S(2)}, u32[]{:S(2)}) async-start(bf16[32,16,768]{2,1,0:T(8,128)(2,1)} %copy-done.2), calls=%async_computation.2 | async-start | bytes 1572864 | tf_op jit(solution)/shard_map/all_to_all | solution.py:491
  111.7 2.2 %collective-permute-start.5 = (bf16[128,1024]{1,0:T(8,128)(2,1)}, bf16[128,1024]{1,0:T(8,128)(2,1)S(1)}, u32[]{:S(2)}, u32[]{:S(2)}) collective-permute-start(bf16[128,1024]{1,0:T(8,128)(2,1)} %keys_values.1.refs_0_), channel_id=1, source_target_pairs={{0,1},{2,3},{6,7},{8,9},{10,11},{12,13},{14,15},{16,17},{18,19},{2... | collective-permute-start | bytes 786440 | tf_op jit(solution)/shard_map/ppermute | solution.py:446
  113.8 1.2 copy-done.1
  115.1 1.0 copy-done.3
  116.1 1.0 queries.1
  117.1 2.0 %collective-permute-done.2.refs_4_ = bf16[128,1024]{1,0:T(8,128)(2,1)} collective-permute-done((bf16[128,1024]{1,0:T(8,128)(2,1)}, bf16[128,1024]{1,0:T(8,128)(2,1)}, u32[]{:S(2)}, u32[]{:S(2)}) %collective-permute-start.2) | collective-permute-done | bytes 262176 | tf_op jit(solution)/shard_map/ppermute | solution.py:444
  119.1 2.8 %collective-permute-done.1.refs_2_ = bf16[128,1024]{1,0:T(8,128)(2,1)} collective-permute-done((bf16[128,1024]{1,0:T(8,128)(2,1)}, bf16[128,1024]{1,0:T(8,128)(2,1)}, u32[]{:S(2)}, u32[]{:S(2)}) %collective-permute-start.1) | collective-permute-done | bytes 262176 | tf_op jit(solution)/shard_map/ppermute | solution.py:444
  121.9 1.9 %collective-permute-start.6 = (bf16[128,1024]{1,0:T(8,128)(2,1)}, bf16[128,1024]{1,0:T(8,128)(2,1)S(1)}, u32[]{:S(2)}, u32[]{:S(2)}) collective-permute-start(bf16[128,1024]{1,0:T(8,128)(2,1)} %collective-permute-done.1.refs_2_), channel_id=1, source_target_pairs={{0,1},{1,0},{2,3},{3,2},{5,4},{7,6},{8,9},{9,8},{10,11},{11,10},{1... | collective-permute-start | bytes 786440 | tf_op jit(solution)/shard_map/ppermute | solution.py:446
  123.8 2.4 %collective-permute-start.7 = (bf16[128,1024]{1,0:T(8,128)(2,1)}, bf16[128,1024]{1,0:T(8,128)(2,1)S(1)}, u32[]{:S(2)}, u32[]{:S(2)}) collective-permute-start(bf16[128,1024]{1,0:T(8,128)(2,1)} %collective-permute-done.2.refs_4_), channel_id=1, source_target_pairs={{0,1},{1,0},{2,3},{3,2},{5,4},{9,8},{10,11},{11,10},{16,17},{17,16... | collective-permute-start | bytes 786440 | tf_op jit(solution)/shard_map/ppermute | solution.py:446
  127.6 5.8 %attend.1 = (bf16[128,2048]{1,0:T(8,128)(2,1)}, bf16[128,2048]{1,0:T(8,128)(2,1)S(1)}) custom-call(s32[1,128]{1,0:T(1,128)S(1)} %broadcast_maximum_fusion.plan_ref, bf16[4,512,128]{2,1,0:T(8,128)(2,1)S(1)} %queries.1, bf16[128,1024]{1,0:T(8,128)(2,1)} %keys_values.1.refs_0_, bf16[128,1024]{1,0:T(8,128)(2,1)S(1)} %collective-permute-done.5.refs_1_, ...), custom_call_target="tpu_custom_call" | custom-call | flops 12000000000 | bytes 8388608 | tf_op jit(solution)/shard_map/attend/pallas_call | solution.py:339
  133.4 3.3 %all-to-all-done.2 = bf16[32,16,768]{2,1,0:T(8,128)(2,1)S(1)} async-done(((bf16[32,16,768]{2,1,0:T(8,128)(2,1)}), bf16[32,16,768]{2,1,0:T(8,128)(2,1)S(1)}, u32[]{:S(2)}, u32[]{:S(2)}) %all-to-all-start.2) | async-done | bytes 786464 | tf_op jit(solution)/shard_map/all_to_all | solution.py:491
  136.7 1.8 %output.1 = bf16[128,4096]{1,0:T(8,128)(2,1)} custom-call(bf16[128,2048]{1,0:T(8,128)(2,1)S(1)} %get-tuple-element.24.attended_ref, bf16[2,16,16,768]{3,2,1,0:T(8,128)(2,1)S(1)} %bitcast.15), custom_call_target="tpu_custom_call" | custom-call | flops 100000000 | bytes 3145728 | tf_op jit(solution)/shard_map/output/pallas_call | solution.py:396
  (34 shorter events, 6.6 us)
Async XLA Ops:
  3.1 7.4 %copy-start.6 = (s32[3]{0:T(128)S(1)}, s32[3]{0:T(128)}, u32[]{:S(2)}) copy-start(s32[3]{0:T(128)} %param.14) | copy-start | bytes 40
  3.1 7.4 %copy-start.7 = (s32[3]{0:T(128)S(1)}, s32[3]{0:T(128)}, u32[]{:S(2)}) copy-start(s32[3]{0:T(128)} %param.13) | copy-start | bytes 40
  3.1 36.0 %all-to-all-start = ((bf16[16,16,2688]{2,1,0:T(8,128)(2,1)}), bf16[16,16,2688]{2,1,0:T(8,128)(2,1)S(1)}, u32[]{:S(2)}, u32[]{:S(2)}) async-start(bf16[16,16,2688]{2,1,0:T(8,128)(2,1)} %bitcast.16), calls=%async_computation | async-start | bytes 2752512 | tf_op jit(solution)/shard_map/all_to_all | solution.py:477
  10.5 3.6 %collective-permute-start = (s32[2,1,3]{2,0,1:T(2,128)S(1)}, s32[2,1,3]{2,0,1:T(2,128)S(1)}, u32[]{:S(2)}, u32[]{:S(2)}) collective-permute-start(s32[2,1,3]{2,0,1:T(2,128)S(1)} %add_bitcast_fusion), channel_id=1, source_target_pairs={{0,16},{16,0},{1,17},{17,1},{2,18},{18,2},{3,19},{19,3},{4,20},{20... | collective-permute-start | bytes 80 | tf_op jit(solution)/shard_map/ppermute | solution.py:481
  39.8 54.9 %copy-start = (bf16[128,4096]{1,0:T(8,128)(2,1)S(1)}, bf16[128,4096]{1,0:T(8,128)(2,1)}, u32[]{:S(2)}) copy-start(bf16[128,4096]{1,0:T(8,128)(2,1)} %hidden_ref.3) | copy-start | bytes 3145732
  39.9 54.9 %copy-start.4 = (bf16[128,512]{1,0:T(8,128)(2,1)S(1)}, bf16[128,512]{1,0:T(8,128)(2,1)}, u32[]{:S(2)}) copy-start(bf16[128,512]{1,0:T(8,128)(2,1)} %key_ref.1) | copy-start | bytes 393220
  39.9 54.9 %copy-start.5 = (bf16[128,512]{1,0:T(8,128)(2,1)S(1)}, bf16[128,512]{1,0:T(8,128)(2,1)}, u32[]{:S(2)}) copy-start(bf16[128,512]{1,0:T(8,128)(2,1)} %value_ref.1) | copy-start | bytes 393220
  96.2 20.9 %collective-permute-start.4 = (bf16[128,1024]{1,0:T(8,128)(2,1)}, bf16[128,1024]{1,0:T(8,128)(2,1)}, u32[]{:S(2)}, u32[]{:S(2)}) collective-permute-start(bf16[128,1024]{1,0:T(8,128)(2,1)} %keys_values.1.refs_0_), channel_id=1, source_target_pairs={{12,4},{13,5},{28,20},{29,21}} | collective-permute-start | bytes 786440 | tf_op jit(solution)/shard_map/ppermute | solution.py:444
  97.5 19.6 %collective-permute-start.3 = (bf16[128,1024]{1,0:T(8,128)(2,1)}, bf16[128,1024]{1,0:T(8,128)(2,1)}, u32[]{:S(2)}, u32[]{:S(2)}) collective-permute-start(bf16[128,1024]{1,0:T(8,128)(2,1)} %keys_values.1.refs_0_), channel_id=1, source_target_pairs={{12,2},{13,3},{14,4},{15,5},{5,11},{28,18},{29,19},{30,20},{31,21}... | collective-permute-start | bytes 786440 | tf_op jit(solution)/shard_map/ppermute | solution.py:444
  98.9 20.2 %collective-permute-start.2 = (bf16[128,1024]{1,0:T(8,128)(2,1)}, bf16[128,1024]{1,0:T(8,128)(2,1)}, u32[]{:S(2)}, u32[]{:S(2)}) collective-permute-start(bf16[128,1024]{1,0:T(8,128)(2,1)} %keys_values.1.refs_0_), channel_id=1, source_target_pairs={{12,0},{13,1},{14,2},{15,3},{0,4},{1,5},{5,9},{6,10},{7,11},{28,16... | collective-permute-start | bytes 786440 | tf_op jit(solution)/shard_map/ppermute | solution.py:444
  101.0 20.9 %collective-permute-start.1 = (bf16[128,1024]{1,0:T(8,128)(2,1)}, bf16[128,1024]{1,0:T(8,128)(2,1)}, u32[]{:S(2)}, u32[]{:S(2)}) collective-permute-start(bf16[128,1024]{1,0:T(8,128)(2,1)} %keys_values.1.refs_0_), channel_id=1, source_target_pairs={{14,0},{15,1},{0,2},{1,3},{2,4},{3,5},{5,7},{6,8},{7,9},{8,10},{9,... | collective-permute-start | bytes 786440 | tf_op jit(solution)/shard_map/ppermute | solution.py:444
  104.3 0.9 copy-start.2
  105.1 31.6 %all-to-all-start.2 = ((bf16[32,16,768]{2,1,0:T(8,128)(2,1)}), bf16[32,16,768]{2,1,0:T(8,128)(2,1)S(1)}, u32[]{:S(2)}, u32[]{:S(2)}) async-start(bf16[32,16,768]{2,1,0:T(8,128)(2,1)} %copy-done.2), calls=%async_computation.2 | async-start | bytes 1572864 | tf_op jit(solution)/shard_map/all_to_all | solution.py:491
  111.7 15.9 %collective-permute-start.5 = (bf16[128,1024]{1,0:T(8,128)(2,1)}, bf16[128,1024]{1,0:T(8,128)(2,1)S(1)}, u32[]{:S(2)}, u32[]{:S(2)}) collective-permute-start(bf16[128,1024]{1,0:T(8,128)(2,1)} %keys_values.1.refs_0_), channel_id=1, source_target_pairs={{0,1},{2,3},{6,7},{8,9},{10,11},{12,13},{14,15},{16,17},{18,19},{2... | collective-permute-start | bytes 786440 | tf_op jit(solution)/shard_map/ppermute | solution.py:446
  113.8 1.2 copy-start.1
  115.1 1.0 copy-start.3
  121.9 5.7 %collective-permute-start.6 = (bf16[128,1024]{1,0:T(8,128)(2,1)}, bf16[128,1024]{1,0:T(8,128)(2,1)S(1)}, u32[]{:S(2)}, u32[]{:S(2)}) collective-permute-start(bf16[128,1024]{1,0:T(8,128)(2,1)} %collective-permute-done.1.refs_2_), channel_id=1, source_target_pairs={{0,1},{1,0},{2,3},{3,2},{5,4},{7,6},{8,9},{9,8},{10,11},{11,10},{1... | collective-permute-start | bytes 786440 | tf_op jit(solution)/shard_map/ppermute | solution.py:446
  123.8 3.8 %collective-permute-start.7 = (bf16[128,1024]{1,0:T(8,128)(2,1)}, bf16[128,1024]{1,0:T(8,128)(2,1)S(1)}, u32[]{:S(2)}, u32[]{:S(2)}) collective-permute-start(bf16[128,1024]{1,0:T(8,128)(2,1)} %collective-permute-done.2.refs_4_), channel_id=1, source_target_pairs={{0,1},{1,0},{2,3},{3,2},{5,4},{9,8},{10,11},{11,10},{16,17},{17,16... | collective-permute-start | bytes 786440 | tf_op jit(solution)/shard_map/ppermute | solution.py:446
  126.2 1.4 %collective-permute-start.8 = (bf16[128,1024]{1,0:T(8,128)(2,1)}, bf16[128,1024]{1,0:T(8,128)(2,1)S(1)}, u32[]{:S(2)}, u32[]{:S(2)}) collective-permute-start(bf16[128,1024]{1,0:T(8,128)(2,1)} %collective-permute-done.3.refs_6_), channel_id=1, source_target_pairs={{2,3},{3,2},{5,4},{11,10},{18,19},{19,18},{21,20},{27,26}} | collective-permute-start | bytes 786440 | tf_op jit(solution)/shard_map/ppermute | solution.py:446
  126.9 0.7 collective-permute-start.9

commit v5 on v4

--- a/solution.py
+++ b/solution.py
@@ -78,13 +78,14 @@
     for which in range(lengths_ref.shape[0]):
         starts, offset = layout(lengths_ref, which, shards)
         entries = [owner_ref[adapters_ref[which, r]] for r in range(len(starts))]
-        at = ENTRY + shards * (own_half if which == 0 else 1 - own_half)
+        halves = lengths_ref.shape[0]
+        half = own_half if which == 0 else 1 - own_half
         for shard in range(shards):
             packed = lax.rem(shard + offset, shards)
             entry = entries[0]
             for start, later in zip(starts[1:], entries[1:]):
                 entry = jnp.where(start <= packed, later, entry)
-            plan = jnp.where(lanes == at + shard, entry, plan)
+            plan = jnp.where(lanes == ENTRY + shard * halves + half, entry, plan)
     out_ref[...] = plan
 
 
@@ -173,9 +174,9 @@
 
 
 def factor(piece_ref, chunk, at, width):
-    halves = piece_ref.shape[0]
+    halves = piece_ref.shape[1]
     place = chunk // halves * ROW_BLOCKS
-    rows = piece_ref[chunk % halves, place : place + ROW_BLOCKS, :, at : at + width]
+    rows = piece_ref[place : place + ROW_BLOCKS, chunk % halves, :, at : at + width]
     return rows.reshape(ROW_BLOCKS * 16, width)
 
 
@@ -355,12 +356,11 @@
 
 def output_kernel(attended_ref, piece_ref, out_ref, down, up, held, in_sem, out_sem):
     q_head, d = down.shape[3], up.shape[3]
-    places = down.shape[1]
-    halves = down.shape[0]
+    halves = down.shape[1]
 
     def take(copy, at, half, index):
-        source = piece_ref.at[half, pl.ds(0, places), :, pl.ds(at, copy.shape[3])]
-        return pltpu.make_async_copy(source, copy.at[half], in_sem.at[index, half])
+        source = piece_ref.at[pl.ds(0, copy.shape[0]), half, :, pl.ds(at, copy.shape[3])]
+        return pltpu.make_async_copy(source, copy.at[:, half], in_sem.at[index, half])
 
     takes = [take(down, 0, h, 0) for h in range(halves)]
     takes_up = [take(up, q_head, h, 1) for h in range(halves)]
@@ -391,7 +391,7 @@
 
 def output_adapter(attended, pieces, model_width):
     tokens, query_width = attended.shape
-    halves, places = pieces.shape[0], pieces.shape[1]
+    places, halves = pieces.shape[0], pieces.shape[1]
     any_space = pl.BlockSpec(memory_space=pl.ANY)
     return pl.pallas_call(
         output_kernel,
@@ -399,8 +399,8 @@
         in_specs=vmem() + [any_space],
         out_specs=any_space,
         scratch_shapes=[
-            pltpu.VMEM((halves, places, 16, query_width // CHUNKS), jnp.bfloat16),
-            pltpu.VMEM((halves, places, 16, model_width // CHUNKS), jnp.bfloat16),
+            pltpu.VMEM((places, halves, 16, query_width // CHUNKS), jnp.bfloat16),
+            pltpu.VMEM((places, halves, 16, model_width // CHUNKS), jnp.bfloat16),
             pltpu.VMEM((tokens, model_width), jnp.bfloat16),
             pltpu.SemaphoreType.DMA((2, halves)),
             pltpu.SemaphoreType.DMA((CHUNKS,)),
@@ -487,9 +487,10 @@
     spread, tables, plan = lax.optimization_barrier((spread, tables, plan))
 
     def collect(pieces):
-        axes = ("groups", "ctx") if halves == 2 else "ctx"
+        axes = ("ctx", "groups") if halves == 2 else "ctx"
         pieces = lax.all_to_all(pieces, axes, split_axis=0, concat_axis=0, tiled=True)
-        return pieces.reshape((halves, shards) + pieces.shape[1:])[:, : ROW_BLOCKS * CHUNKS]
+        pieces = pieces.reshape((shards, halves) + pieces.shape[1:])
+        return pieces[: ROW_BLOCKS * CHUNKS // halves]
 
     kv_width, q_width, o_width = parts.widths
     dests = shards * halves

time: 139 us -> 141 us (1.014)
    ppermute x4, waiting for transfers between devices: 4.79 us -> 6.77 us  [exchange(): lax.ppermute(kv, 'ctx', shift_pairs(shards, s))]
  transfers between devices with their start and end apart: 12 -> 12, of which waited for: 5 -> 6; matrix products, arithmetic and copies ran while one was open for 2% -> 2% of each run, Pallas kernels for 6% -> 6%
where the time goes in v5:
time: 141 us; the launch traced here: 139 us
  blocking collectives  53.9 us (38%)
  starting transfers between devices  31.5 us (22%)
  waiting for transfers between devices  31.2 us (22%)
  Pallas kernels  15.3 us (11%)
  local copies, waits for them, and re-layouts  3.75 us (3%)
  other arithmetic  2.28 us (2%)
  between operations  1.53 us (1%)
    all_to_all x1, blocking collectives, collect(): lax.all_to_all(pieces, axes, split_axis=0, concat_axis=0, tiled=True)  53.9 us
    all_to_all x1, waiting for transfers between devices, body(): lax.all_to_all(packed, 'ctx', split_axis=0, concat_axis=0, tiled=True)  20.7 us
    ppermute x5, starting transfers between devices, exchange(): lax.ppermute(b, 'ctx', swap_pairs(shards, s))  7.84 us
    all_to_all x1, starting transfers between devices, collect(): lax.all_to_all(pieces, axes, split_axis=0, concat_axis=0, tiled=True)  7.4 us
    all_to_all x1, starting transfers between devices, body(): lax.all_to_all(packed, 'ctx', split_axis=0, concat_axis=0, tiled=True)  7.4 us
    ppermute x4, starting transfers between devices, exchange(): lax.ppermute(kv, 'ctx', shift_pairs(shards, s))  7.32 us
    ppermute x4, waiting for transfers between devices, exchange(): lax.ppermute(kv, 'ctx', shift_pairs(shards, s))  6.77 us
    pallas_call x1, Pallas kernels, attend(): pl.pallas_call(functools.partial(attend_kernel, steps), out_shape=[jax.Sh...  5.76 us
  transfers between devices with their start and end apart: 12, of which 6 were waited for; matrix products, arithmetic and copies ran while one was open for 2% of the time, Pallas kernels for 6%

profile of v5, /device:TPU:0, one launch (start us, length us, event | category | flops | bytes accessed | tf_op | source)
XLA Modules:
  0.0 139.4 jit_solution(15940450311538212309)
XLA Ops:
  0.6 2.4 %pack.1 = bf16[1,4,4,16,2688]{4,3,2,1,0:T(8,128)(2,1)} custom-call(bf16[4,16,21504]{2,1,0:T(8,128)(2,1)} %bitcast.17), custom_call_target="tpu_custom_call" | custom-call | tf_op jit(solution)/shard_map/pack/pallas_call | solution.py:138
  3.1 7.4 %all-to-all-start = ((bf16[16,16,2688]{2,1,0:T(8,128)(2,1)}), bf16[16,16,2688]{2,1,0:T(8,128)(2,1)S(1)}, u32[]{:S(2)}, u32[]{:S(2)}) async-start(bf16[16,16,2688]{2,1,0:T(8,128)(2,1)} %bitcast.16), calls=%async_computation | async-start | bytes 2752512 | tf_op jit(solution)/shard_map/all_to_all | solution.py:477
  10.5 1.6 %collective-permute-start = (s32[2,1,3]{2,0,1:T(2,128)S(1)}, s32[2,1,3]{2,0,1:T(2,128)S(1)}, u32[]{:S(2)}, u32[]{:S(2)}) collective-permute-start(s32[2,1,3]{2,0,1:T(2,128)S(1)} %add_bitcast_fusion), channel_id=1, source_target_pairs={{0,16},{16,0},{1,17},{17,1},{2,18},{18,2},{3,19},{19,3},{4,20},{20... | collective-permute-start | bytes 80 | tf_op jit(solution)/shard_map/ppermute | solution.py:481
  12.8 1.4 collective-permute-done
  14.7 1.4 plan.1
  18.4 20.7 %all-to-all-done.spread_ref = bf16[16,16,2688]{2,1,0:T(8,128)(2,1)S(1)} async-done(((bf16[16,16,2688]{2,1,0:T(8,128)(2,1)}), bf16[16,16,2688]{2,1,0:T(8,128)(2,1)S(1)}, u32[]{:S(2)}, u32[]{:S(2)}) %all-to-all-start) | async-done | bytes 1376288 | tf_op jit(solution)/shard_map/all_to_all | solution.py:477
  39.9 53.9 %all_to_all.15 = bf16[32,16,1920]{2,1,0:T(8,128)(2,1)S(1)} all-to-all(bf16[32,16,1920]{2,1,0:T(8,128)(2,1)S(1)} %route.2), channel_id=1, replica_groups=mesh['groups'=2,'ctx'=16] {'ctx','groups'}, dimensions={0} | all-to-all | bytes 3932160 | tf_op jit(solution)/shard_map/all_to_all | solution.py:491
  93.8 1.5 %keys_values.1.refs_0_ = bf16[128,1024]{1,0:T(8,128)(2,1)} custom-call(bf16[128,4096]{1,0:T(8,128)(2,1)S(1)} %copy-done, bf16[128,512]{1,0:T(8,128)(2,1)S(1)} %copy-done.4, bf16[128,512]{1,0:T(8,128)(2,1)S(1)} %copy-done.5, f32[128,128]{1,0:T(8,128)S(1)} %get-tuple-element.15.cos_ref, f32[128,128]{1,0:T(8,128)S(1)} %get-tuple-element.16.sin_ref, ...), custom_call_target="tpu_custom_call" | custom-call | flops 150000000 | bytes 3145728 | tf_op jit(solution)/shard_map/keys_values/pallas_call | solution.py:220
  95.3 1.4 collective-permute-start.4
  96.6 1.4 collective-permute-start.3
  98.0 2.2 %collective-permute-start.2 = (bf16[128,1024]{1,0:T(8,128)(2,1)}, bf16[128,1024]{1,0:T(8,128)(2,1)}, u32[]{:S(2)}, u32[]{:S(2)}) collective-permute-start(bf16[128,1024]{1,0:T(8,128)(2,1)} %keys_values.1.refs_0_), channel_id=1, source_target_pairs={{12,0},{13,1},{14,2},{15,3},{0,4},{1,5},{5,9},{6,10},{7,11},{28,16... | collective-permute-start | bytes 786440 | tf_op jit(solution)/shard_map/ppermute | solution.py:444
  100.1 2.4 %collective-permute-start.1 = (bf16[128,1024]{1,0:T(8,128)(2,1)}, bf16[128,1024]{1,0:T(8,128)(2,1)}, u32[]{:S(2)}, u32[]{:S(2)}) collective-permute-start(bf16[128,1024]{1,0:T(8,128)(2,1)} %keys_values.1.refs_0_), channel_id=1, source_target_pairs={{14,0},{15,1},{0,2},{1,3},{2,4},{3,5},{5,7},{6,8},{7,9},{8,10},{9,... | collective-permute-start | bytes 786440 | tf_op jit(solution)/shard_map/ppermute | solution.py:444
  104.2 7.4 %all-to-all-start.2 = ((bf16[32,16,768]{2,1,0:T(8,128)(2,1)}), bf16[32,16,768]{2,1,0:T(8,128)(2,1)S(1)}, u32[]{:S(2)}, u32[]{:S(2)}) async-start(bf16[32,16,768]{2,1,0:T(8,128)(2,1)} %copy-done.2), calls=%async_computation.2 | async-start | bytes 1572864 | tf_op jit(solution)/shard_map/all_to_all | solution.py:491
  111.6 2.2 %collective-permute-start.5 = (bf16[128,1024]{1,0:T(8,128)(2,1)}, bf16[128,1024]{1,0:T(8,128)(2,1)S(1)}, u32[]{:S(2)}, u32[]{:S(2)}) collective-permute-start(bf16[128,1024]{1,0:T(8,128)(2,1)} %keys_values.1.refs_0_), channel_id=1, source_target_pairs={{0,1},{2,3},{6,7},{8,9},{10,11},{12,13},{14,15},{16,17},{18,19},{2... | collective-permute-start | bytes 786440 | tf_op jit(solution)/shard_map/ppermute | solution.py:446
  113.8 1.2 copy-done.1
  115.0 1.0 copy-done.3
  116.0 1.0 queries.1
  117.0 1.2 collective-permute-done.2.refs_4_
  118.2 5.6 %collective-permute-done.1.refs_2_ = bf16[128,1024]{1,0:T(8,128)(2,1)} collective-permute-done((bf16[128,1024]{1,0:T(8,128)(2,1)}, bf16[128,1024]{1,0:T(8,128)(2,1)}, u32[]{:S(2)}, u32[]{:S(2)}) %collective-permute-start.1) | collective-permute-done | bytes 262176 | tf_op jit(solution)/shard_map/ppermute | solution.py:444
  123.8 2.4 %collective-permute-start.6 = (bf16[128,1024]{1,0:T(8,128)(2,1)}, bf16[128,1024]{1,0:T(8,128)(2,1)S(1)}, u32[]{:S(2)}, u32[]{:S(2)}) collective-permute-start(bf16[128,1024]{1,0:T(8,128)(2,1)} %collective-permute-done.1.refs_2_), channel_id=1, source_target_pairs={{0,1},{1,0},{2,3},{3,2},{5,4},{7,6},{8,9},{9,8},{10,11},{11,10},{1... | collective-permute-start | bytes 786440 | tf_op jit(solution)/shard_map/ppermute | solution.py:446
  126.2 1.9 %collective-permute-start.7 = (bf16[128,1024]{1,0:T(8,128)(2,1)}, bf16[128,1024]{1,0:T(8,128)(2,1)S(1)}, u32[]{:S(2)}, u32[]{:S(2)}) collective-permute-start(bf16[128,1024]{1,0:T(8,128)(2,1)} %collective-permute-done.2.refs_4_), channel_id=1, source_target_pairs={{0,1},{1,0},{2,3},{3,2},{5,4},{9,8},{10,11},{11,10},{16,17},{17,16... | collective-permute-start | bytes 786440 | tf_op jit(solution)/shard_map/ppermute | solution.py:446
  129.9 5.8 %attend.1 = (bf16[128,2048]{1,0:T(8,128)(2,1)}, bf16[128,2048]{1,0:T(8,128)(2,1)S(1)}) custom-call(s32[1,128]{1,0:T(1,128)S(1)} %broadcast_maximum_fusion.plan_ref, bf16[4,512,128]{2,1,0:T(8,128)(2,1)S(1)} %queries.1, bf16[128,1024]{1,0:T(8,128)(2,1)} %keys_values.1.refs_0_, bf16[128,1024]{1,0:T(8,128)(2,1)S(1)} %collective-permute-done.5.refs_1_, ...), custom_call_target="tpu_custom_call" | custom-call | flops 12000000000 | bytes 8388608 | tf_op jit(solution)/shard_map/attend/pallas_call | solution.py:340
  135.6 2.0 %all-to-all-done.2 = bf16[32,16,768]{2,1,0:T(8,128)(2,1)S(1)} async-done(((bf16[32,16,768]{2,1,0:T(8,128)(2,1)}), bf16[32,16,768]{2,1,0:T(8,128)(2,1)S(1)}, u32[]{:S(2)}, u32[]{:S(2)}) %all-to-all-start.2) | async-done | bytes 786464 | tf_op jit(solution)/shard_map/all_to_all | solution.py:491
  137.6 1.8 %output.1 = bf16[128,4096]{1,0:T(8,128)(2,1)} custom-call(bf16[128,2048]{1,0:T(8,128)(2,1)S(1)} %get-tuple-element.24.attended_ref, bf16[16,2,16,768]{3,2,1,0:T(8,128)(2,1)S(1)} %bitcast.15), custom_call_target="tpu_custom_call" | custom-call | flops 100000000 | bytes 3145728 | tf_op jit(solution)/shard_map/output/pallas_call | solution.py:396
  (34 shorter events, 6.9 us)
Async XLA Ops:
  3.1 7.4 %copy-start.6 = (s32[3]{0:T(128)S(1)}, s32[3]{0:T(128)}, u32[]{:S(2)}) copy-start(s32[3]{0:T(128)} %param.14) | copy-start | bytes 40
  3.1 7.4 %copy-start.7 = (s32[3]{0:T(128)S(1)}, s32[3]{0:T(128)}, u32[]{:S(2)}) copy-start(s32[3]{0:T(128)} %param.13) | copy-start | bytes 40
  3.1 36.0 %all-to-all-start = ((bf16[16,16,2688]{2,1,0:T(8,128)(2,1)}), bf16[16,16,2688]{2,1,0:T(8,128)(2,1)S(1)}, u32[]{:S(2)}, u32[]{:S(2)}) async-start(bf16[16,16,2688]{2,1,0:T(8,128)(2,1)} %bitcast.16), calls=%async_computation | async-start | bytes 2752512 | tf_op jit(solution)/shard_map/all_to_all | solution.py:477
  10.5 3.6 %collective-permute-start = (s32[2,1,3]{2,0,1:T(2,128)S(1)}, s32[2,1,3]{2,0,1:T(2,128)S(1)}, u32[]{:S(2)}, u32[]{:S(2)}) collective-permute-start(s32[2,1,3]{2,0,1:T(2,128)S(1)} %add_bitcast_fusion), channel_id=1, source_target_pairs={{0,16},{16,0},{1,17},{17,1},{2,18},{18,2},{3,19},{19,3},{4,20},{20... | collective-permute-start | bytes 80 | tf_op jit(solution)/shard_map/ppermute | solution.py:481
  39.8 53.9 %copy-start = (bf16[128,4096]{1,0:T(8,128)(2,1)S(1)}, bf16[128,4096]{1,0:T(8,128)(2,1)}, u32[]{:S(2)}) copy-start(bf16[128,4096]{1,0:T(8,128)(2,1)} %hidden_ref.3) | copy-start | bytes 3145732
  39.9 53.9 %copy-start.4 = (bf16[128,512]{1,0:T(8,128)(2,1)S(1)}, bf16[128,512]{1,0:T(8,128)(2,1)}, u32[]{:S(2)}) copy-start(bf16[128,512]{1,0:T(8,128)(2,1)} %key_ref.1) | copy-start | bytes 393220
  39.9 53.9 %copy-start.5 = (bf16[128,512]{1,0:T(8,128)(2,1)S(1)}, bf16[128,512]{1,0:T(8,128)(2,1)}, u32[]{:S(2)}) copy-start(bf16[128,512]{1,0:T(8,128)(2,1)} %value_ref.1) | copy-start | bytes 393220
  95.3 21.8 %collective-permute-start.4 = (bf16[128,1024]{1,0:T(8,128)(2,1)}, bf16[128,1024]{1,0:T(8,128)(2,1)}, u32[]{:S(2)}, u32[]{:S(2)}) collective-permute-start(bf16[128,1024]{1,0:T(8,128)(2,1)} %keys_values.1.refs_0_), channel_id=1, source_target_pairs={{12,4},{13,5},{28,20},{29,21}} | collective-permute-start | bytes 786440 | tf_op jit(solution)/shard_map/ppermute | solution.py:444
  96.6 20.4 %collective-permute-start.3 = (bf16[128,1024]{1,0:T(8,128)(2,1)}, bf16[128,1024]{1,0:T(8,128)(2,1)}, u32[]{:S(2)}, u32[]{:S(2)}) collective-permute-start(bf16[128,1024]{1,0:T(8,128)(2,1)} %keys_values.1.refs_0_), channel_id=1, source_target_pairs={{12,2},{13,3},{14,4},{15,5},{5,11},{28,18},{29,19},{30,20},{31,21}... | collective-permute-start | bytes 786440 | tf_op jit(solution)/shard_map/ppermute | solution.py:444
  98.0 20.2 %collective-permute-start.2 = (bf16[128,1024]{1,0:T(8,128)(2,1)}, bf16[128,1024]{1,0:T(8,128)(2,1)}, u32[]{:S(2)}, u32[]{:S(2)}) collective-permute-start(bf16[128,1024]{1,0:T(8,128)(2,1)} %keys_values.1.refs_0_), channel_id=1, source_target_pairs={{12,0},{13,1},{14,2},{15,3},{0,4},{1,5},{5,9},{6,10},{7,11},{28,16... | collective-permute-start | bytes 786440 | tf_op jit(solution)/shard_map/ppermute | solution.py:444
  100.1 23.7 %collective-permute-start.1 = (bf16[128,1024]{1,0:T(8,128)(2,1)}, bf16[128,1024]{1,0:T(8,128)(2,1)}, u32[]{:S(2)}, u32[]{:S(2)}) collective-permute-start(bf16[128,1024]{1,0:T(8,128)(2,1)} %keys_values.1.refs_0_), channel_id=1, source_target_pairs={{14,0},{15,1},{0,2},{1,3},{2,4},{3,5},{5,7},{6,8},{7,9},{8,10},{9,... | collective-permute-start | bytes 786440 | tf_op jit(solution)/shard_map/ppermute | solution.py:444
  103.3 0.9 copy-start.2
  104.2 33.4 %all-to-all-start.2 = ((bf16[32,16,768]{2,1,0:T(8,128)(2,1)}), bf16[32,16,768]{2,1,0:T(8,128)(2,1)S(1)}, u32[]{:S(2)}, u32[]{:S(2)}) async-start(bf16[32,16,768]{2,1,0:T(8,128)(2,1)} %copy-done.2), calls=%async_computation.2 | async-start | bytes 1572864 | tf_op jit(solution)/shard_map/all_to_all | solution.py:491
  111.6 17.9 %collective-permute-start.5 = (bf16[128,1024]{1,0:T(8,128)(2,1)}, bf16[128,1024]{1,0:T(8,128)(2,1)S(1)}, u32[]{:S(2)}, u32[]{:S(2)}) collective-permute-start(bf16[128,1024]{1,0:T(8,128)(2,1)} %keys_values.1.refs_0_), channel_id=1, source_target_pairs={{0,1},{2,3},{6,7},{8,9},{10,11},{12,13},{14,15},{16,17},{18,19},{2... | collective-permute-start | bytes 786440 | tf_op jit(solution)/shard_map/ppermute | solution.py:446
  113.8 1.2 copy-start.1
  115.0 1.0 copy-start.3
  123.8 5.7 %collective-permute-start.6 = (bf16[128,1024]{1,0:T(8,128)(2,1)}, bf16[128,1024]{1,0:T(8,128)(2,1)S(1)}, u32[]{:S(2)}, u32[]{:S(2)}) collective-permute-start(bf16[128,1024]{1,0:T(8,128)(2,1)} %collective-permute-done.1.refs_2_), channel_id=1, source_target_pairs={{0,1},{1,0},{2,3},{3,2},{5,4},{7,6},{8,9},{9,8},{10,11},{11,10},{1... | collective-permute-start | bytes 786440 | tf_op jit(solution)/shard_map/ppermute | solution.py:446
  126.2 3.6 %collective-permute-start.7 = (bf16[128,1024]{1,0:T(8,128)(2,1)}, bf16[128,1024]{1,0:T(8,128)(2,1)S(1)}, u32[]{:S(2)}, u32[]{:S(2)}) collective-permute-start(bf16[128,1024]{1,0:T(8,128)(2,1)} %collective-permute-done.2.refs_4_), channel_id=1, source_target_pairs={{0,1},{1,0},{2,3},{3,2},{5,4},{9,8},{10,11},{11,10},{16,17},{17,16... | collective-permute-start | bytes 786440 | tf_op jit(solution)/shard_map/ppermute | solution.py:446
  128.1 1.7 %collective-permute-start.8 = (bf16[128,1024]{1,0:T(8,128)(2,1)}, bf16[128,1024]{1,0:T(8,128)(2,1)S(1)}, u32[]{:S(2)}, u32[]{:S(2)}) collective-permute-start(bf16[128,1024]{1,0:T(8,128)(2,1)} %collective-permute-done.3.refs_6_), channel_id=1, source_target_pairs={{2,3},{3,2},{5,4},{11,10},{18,19},{19,18},{21,20},{27,26}} | collective-permute-start | bytes 786440 | tf_op jit(solution)/shard_map/ppermute | solution.py:446
  128.8 1.0 collective-permute-start.9

commit v6 on v4

--- a/solution.py
+++ b/solution.py
@@ -441,7 +441,8 @@
 
 def exchange(kv, queries, shards, reach):
     shifts = range(0, reach + 1, 2)
-    got = [kv] + [lax.ppermute(kv, "ctx", shift_pairs(shards, s)) for s in shifts[1:]]
+    far = [lax.ppermute(kv, "ctx", shift_pairs(shards, s)) for s in reversed(shifts[1:])]
+    got = [kv] + far[::-1]
     got[1:], queries = lax.optimization_barrier((got[1:], queries))
     swapped = [lax.ppermute(b, "ctx", swap_pairs(shards, s)) for s, b in zip(shifts, got)]
     blocks, steps = [kv], [(0, True)]

time: 139 us -> 139 us (level)
  no operation moved by 1% of the time
where the time goes in v6:
time: 139 us
  blocking collectives  54.8 us (39%)
  starting transfers between devices  30.6 us (22%)
  waiting for transfers between devices  30.2 us (22%)
  Pallas kernels  15.3 us (11%)
  local copies, waits for them, and re-layouts  3.75 us (3%)
  other arithmetic  2.28 us (2%)
  between operations  1.55 us (1%)
    all_to_all x1, blocking collectives, collect(): lax.all_to_all(pieces, axes, split_axis=0, concat_axis=0, tiled=True)  54.8 us
    all_to_all x1, waiting for transfers between devices, body(): lax.all_to_all(packed, 'ctx', split_axis=0, concat_axis=0, tiled=True)  20.7 us
    ppermute x5, starting transfers between devices, exchange(): lax.ppermute(b, 'ctx', swap_pairs(shards, s))  7.84 us
    all_to_all x1, starting transfers between devices, body(): lax.all_to_all(packed, 'ctx', split_axis=0, concat_axis=0, tiled=True)  7.4 us
    ppermute x4, starting transfers between devices, exchange(): lax.ppermute(kv, 'ctx', shift_pairs(shards, s))  7.33 us
    all_to_all x1, starting transfers between devices, collect(): lax.all_to_all(pieces, axes, split_axis=0, concat_axis=0, tiled=True)  6.5 us
    pallas_call x1, Pallas kernels, attend(): pl.pallas_call(functools.partial(attend_kernel, steps), out_shape=[jax.Sh...  5.77 us
    ppermute x4, waiting for transfers between devices, exchange(): lax.ppermute(kv, 'ctx', shift_pairs(shards, s))  4.79 us
  transfers between devices with their start and end apart: 12, of which 5 were waited for; matrix products, arithmetic and copies ran while one was open for 2% of the time, Pallas kernels for 6%

profile of v6, /device:TPU:0, one launch (start us, length us, event | category | flops | bytes accessed | tf_op | source)
XLA Modules:
  0.0 138.5 jit_solution(11669697696093033827)
XLA Ops:
  0.6 2.4 %pack.1 = bf16[1,4,4,16,2688]{4,3,2,1,0:T(8,128)(2,1)} custom-call(bf16[4,16,21504]{2,1,0:T(8,128)(2,1)} %bitcast.17), custom_call_target="tpu_custom_call" | custom-call | tf_op jit(solution)/shard_map/pack/pallas_call | solution.py:137
  3.1 7.4 %all-to-all-start = ((bf16[16,16,2688]{2,1,0:T(8,128)(2,1)}), bf16[16,16,2688]{2,1,0:T(8,128)(2,1)S(1)}, u32[]{:S(2)}, u32[]{:S(2)}) async-start(bf16[16,16,2688]{2,1,0:T(8,128)(2,1)} %bitcast.16), calls=%async_computation | async-start | bytes 2752512 | tf_op jit(solution)/shard_map/all_to_all | solution.py:478
  10.5 1.6 %collective-permute-start = (s32[2,1,3]{2,0,1:T(2,128)S(1)}, s32[2,1,3]{2,0,1:T(2,128)S(1)}, u32[]{:S(2)}, u32[]{:S(2)}) collective-permute-start(s32[2,1,3]{2,0,1:T(2,128)S(1)} %add_bitcast_fusion), channel_id=1, source_target_pairs={{0,16},{16,0},{1,17},{17,1},{2,18},{18,2},{3,19},{19,3},{4,20},{20... | collective-permute-start | bytes 80 | tf_op jit(solution)/shard_map/ppermute | solution.py:482
  12.8 1.4 %collective-permute-done = s32[2,1,3]{2,0,1:T(2,128)S(1)} collective-permute-done((s32[2,1,3]{2,0,1:T(2,128)S(1)}, s32[2,1,3]{2,0,1:T(2,128)S(1)}, u32[]{:S(2)}, u32[]{:S(2)}) %collective-permute-start) | collective-permute-done | bytes 56 | tf_op jit(solution)/shard_map/ppermute | solution.py:482
  14.7 1.4 plan.1
  18.4 20.7 %all-to-all-done.spread_ref = bf16[16,16,2688]{2,1,0:T(8,128)(2,1)S(1)} async-done(((bf16[16,16,2688]{2,1,0:T(8,128)(2,1)}), bf16[16,16,2688]{2,1,0:T(8,128)(2,1)S(1)}, u32[]{:S(2)}, u32[]{:S(2)}) %all-to-all-start) | async-done | bytes 1376288 | tf_op jit(solution)/shard_map/all_to_all | solution.py:478
  39.9 54.8 %all_to_all.15 = bf16[32,16,1920]{2,1,0:T(8,128)(2,1)S(1)} all-to-all(bf16[32,16,1920]{2,1,0:T(8,128)(2,1)S(1)} %route.2), channel_id=1, replica_groups=mesh['groups'=2,'ctx'=16] {'groups','ctx'}, dimensions={0} | all-to-all | bytes 3932160 | tf_op jit(solution)/shard_map/all_to_all | solution.py:492
  94.7 1.5 %keys_values.1.refs_0_ = bf16[128,1024]{1,0:T(8,128)(2,1)} custom-call(bf16[128,4096]{1,0:T(8,128)(2,1)S(1)} %copy-done, bf16[128,512]{1,0:T(8,128)(2,1)S(1)} %copy-done.4, bf16[128,512]{1,0:T(8,128)(2,1)S(1)} %copy-done.5, f32[128,128]{1,0:T(8,128)S(1)} %get-tuple-element.15.cos_ref, f32[128,128]{1,0:T(8,128)S(1)} %get-tuple-element.16.sin_ref, ...), custom_call_target="tpu_custom_call" | custom-call | flops 150000000 | bytes 3145728 | tf_op jit(solution)/shard_map/keys_values/pallas_call | solution.py:219
  96.2 1.4 collective-permute-start.4
  97.5 1.4 collective-permute-start.3
  98.9 2.0 %collective-permute-start.2 = (bf16[128,1024]{1,0:T(8,128)(2,1)}, bf16[128,1024]{1,0:T(8,128)(2,1)}, u32[]{:S(2)}, u32[]{:S(2)}) collective-permute-start(bf16[128,1024]{1,0:T(8,128)(2,1)} %keys_values.1.refs_0_), channel_id=1, source_target_pairs={{12,0},{13,1},{14,2},{15,3},{0,4},{1,5},{5,9},{6,10},{7,11},{28,16... | collective-permute-start | bytes 786440 | tf_op jit(solution)/shard_map/ppermute | solution.py:444
  101.0 2.6 %collective-permute-start.1 = (bf16[128,1024]{1,0:T(8,128)(2,1)}, bf16[128,1024]{1,0:T(8,128)(2,1)}, u32[]{:S(2)}, u32[]{:S(2)}) collective-permute-start(bf16[128,1024]{1,0:T(8,128)(2,1)} %keys_values.1.refs_0_), channel_id=1, source_target_pairs={{14,0},{15,1},{0,2},{1,3},{2,4},{3,5},{5,7},{6,8},{7,9},{8,10},{9,... | collective-permute-start | bytes 786440 | tf_op jit(solution)/shard_map/ppermute | solution.py:444
  105.1 6.5 %all-to-all-start.2 = ((bf16[32,16,768]{2,1,0:T(8,128)(2,1)}), bf16[32,16,768]{2,1,0:T(8,128)(2,1)S(1)}, u32[]{:S(2)}, u32[]{:S(2)}) async-start(bf16[32,16,768]{2,1,0:T(8,128)(2,1)} %copy-done.2), calls=%async_computation.2 | async-start | bytes 1572864 | tf_op jit(solution)/shard_map/all_to_all | solution.py:492
  111.7 2.2 %collective-permute-start.5 = (bf16[128,1024]{1,0:T(8,128)(2,1)}, bf16[128,1024]{1,0:T(8,128)(2,1)S(1)}, u32[]{:S(2)}, u32[]{:S(2)}) collective-permute-start(bf16[128,1024]{1,0:T(8,128)(2,1)} %keys_values.1.refs_0_), channel_id=1, source_target_pairs={{0,1},{2,3},{6,7},{8,9},{10,11},{12,13},{14,15},{16,17},{18,19},{2... | collective-permute-start | bytes 786440 | tf_op jit(solution)/shard_map/ppermute | solution.py:447
  113.8 1.2 copy-done.1
  115.1 1.0 copy-done.3
  116.1 1.0 queries.1
  117.1 2.0 %collective-permute-done.2.refs_4_ = bf16[128,1024]{1,0:T(8,128)(2,1)} collective-permute-done((bf16[128,1024]{1,0:T(8,128)(2,1)}, bf16[128,1024]{1,0:T(8,128)(2,1)}, u32[]{:S(2)}, u32[]{:S(2)}) %collective-permute-start.2) | collective-permute-done | bytes 262176 | tf_op jit(solution)/shard_map/ppermute | solution.py:444
  119.1 2.8 %collective-permute-done.1.refs_2_ = bf16[128,1024]{1,0:T(8,128)(2,1)} collective-permute-done((bf16[128,1024]{1,0:T(8,128)(2,1)}, bf16[128,1024]{1,0:T(8,128)(2,1)}, u32[]{:S(2)}, u32[]{:S(2)}) %collective-permute-start.1) | collective-permute-done | bytes 262176 | tf_op jit(solution)/shard_map/ppermute | solution.py:444
  121.9 1.9 %collective-permute-start.6 = (bf16[128,1024]{1,0:T(8,128)(2,1)}, bf16[128,1024]{1,0:T(8,128)(2,1)S(1)}, u32[]{:S(2)}, u32[]{:S(2)}) collective-permute-start(bf16[128,1024]{1,0:T(8,128)(2,1)} %collective-permute-done.1.refs_2_), channel_id=1, source_target_pairs={{0,1},{1,0},{2,3},{3,2},{5,4},{7,6},{8,9},{9,8},{10,11},{11,10},{1... | collective-permute-start | bytes 786440 | tf_op jit(solution)/shard_map/ppermute | solution.py:447
  123.8 2.4 %collective-permute-start.7 = (bf16[128,1024]{1,0:T(8,128)(2,1)}, bf16[128,1024]{1,0:T(8,128)(2,1)S(1)}, u32[]{:S(2)}, u32[]{:S(2)}) collective-permute-start(bf16[128,1024]{1,0:T(8,128)(2,1)} %collective-permute-done.2.refs_4_), channel_id=1, source_target_pairs={{0,1},{1,0},{2,3},{3,2},{5,4},{9,8},{10,11},{11,10},{16,17},{17,16... | collective-permute-start | bytes 786440 | tf_op jit(solution)/shard_map/ppermute | solution.py:447
  127.6 5.8 %attend.1 = (bf16[128,2048]{1,0:T(8,128)(2,1)}, bf16[128,2048]{1,0:T(8,128)(2,1)S(1)}) custom-call(s32[1,128]{1,0:T(1,128)S(1)} %broadcast_maximum_fusion.plan_ref, bf16[4,512,128]{2,1,0:T(8,128)(2,1)S(1)} %queries.1, bf16[128,1024]{1,0:T(8,128)(2,1)} %keys_values.1.refs_0_, bf16[128,1024]{1,0:T(8,128)(2,1)S(1)} %collective-permute-done.5.refs_1_, ...), custom_call_target="tpu_custom_call" | custom-call | flops 12000000000 | bytes 8388608 | tf_op jit(solution)/shard_map/attend/pallas_call | solution.py:339
  133.4 3.3 %all-to-all-done.2 = bf16[32,16,768]{2,1,0:T(8,128)(2,1)S(1)} async-done(((bf16[32,16,768]{2,1,0:T(8,128)(2,1)}), bf16[32,16,768]{2,1,0:T(8,128)(2,1)S(1)}, u32[]{:S(2)}, u32[]{:S(2)}) %all-to-all-start.2) | async-done | bytes 786464 | tf_op jit(solution)/shard_map/all_to_all | solution.py:492
  136.7 1.8 %output.1 = bf16[128,4096]{1,0:T(8,128)(2,1)} custom-call(bf16[128,2048]{1,0:T(8,128)(2,1)S(1)} %get-tuple-element.24.attended_ref, bf16[2,16,16,768]{3,2,1,0:T(8,128)(2,1)S(1)} %bitcast.15), custom_call_target="tpu_custom_call" | custom-call | flops 100000000 | bytes 3145728 | tf_op jit(solution)/shard_map/output/pallas_call | solution.py:396
  (34 shorter events, 6.6 us)
Async XLA Ops:
  3.1 7.4 %copy-start.6 = (s32[3]{0:T(128)S(1)}, s32[3]{0:T(128)}, u32[]{:S(2)}) copy-start(s32[3]{0:T(128)} %param.14) | copy-start | bytes 40
  3.1 7.4 %copy-start.7 = (s32[3]{0:T(128)S(1)}, s32[3]{0:T(128)}, u32[]{:S(2)}) copy-start(s32[3]{0:T(128)} %param.13) | copy-start | bytes 40
  3.1 36.0 %all-to-all-start = ((bf16[16,16,2688]{2,1,0:T(8,128)(2,1)}), bf16[16,16,2688]{2,1,0:T(8,128)(2,1)S(1)}, u32[]{:S(2)}, u32[]{:S(2)}) async-start(bf16[16,16,2688]{2,1,0:T(8,128)(2,1)} %bitcast.16), calls=%async_computation | async-start | bytes 2752512 | tf_op jit(solution)/shard_map/all_to_all | solution.py:478
  10.5 3.6 %collective-permute-start = (s32[2,1,3]{2,0,1:T(2,128)S(1)}, s32[2,1,3]{2,0,1:T(2,128)S(1)}, u32[]{:S(2)}, u32[]{:S(2)}) collective-permute-start(s32[2,1,3]{2,0,1:T(2,128)S(1)} %add_bitcast_fusion), channel_id=1, source_target_pairs={{0,16},{16,0},{1,17},{17,1},{2,18},{18,2},{3,19},{19,3},{4,20},{20... | collective-permute-start | bytes 80 | tf_op jit(solution)/shard_map/ppermute | solution.py:482
  39.8 54.9 %copy-start = (bf16[128,4096]{1,0:T(8,128)(2,1)S(1)}, bf16[128,4096]{1,0:T(8,128)(2,1)}, u32[]{:S(2)}) copy-start(bf16[128,4096]{1,0:T(8,128)(2,1)} %hidden_ref.3) | copy-start | bytes 3145732
  39.9 54.9 %copy-start.4 = (bf16[128,512]{1,0:T(8,128)(2,1)S(1)}, bf16[128,512]{1,0:T(8,128)(2,1)}, u32[]{:S(2)}) copy-start(bf16[128,512]{1,0:T(8,128)(2,1)} %key_ref.1) | copy-start | bytes 393220
  39.9 54.9 %copy-start.5 = (bf16[128,512]{1,0:T(8,128)(2,1)S(1)}, bf16[128,512]{1,0:T(8,128)(2,1)}, u32[]{:S(2)}) copy-start(bf16[128,512]{1,0:T(8,128)(2,1)} %value_ref.1) | copy-start | bytes 393220
  96.2 20.9 %collective-permute-start.4 = (bf16[128,1024]{1,0:T(8,128)(2,1)}, bf16[128,1024]{1,0:T(8,128)(2,1)}, u32[]{:S(2)}, u32[]{:S(2)}) collective-permute-start(bf16[128,1024]{1,0:T(8,128)(2,1)} %keys_values.1.refs_0_), channel_id=1, source_target_pairs={{12,4},{13,5},{28,20},{29,21}} | collective-permute-start | bytes 786440 | tf_op jit(solution)/shard_map/ppermute | solution.py:444
  97.5 19.6 %collective-permute-start.3 = (bf16[128,1024]{1,0:T(8,128)(2,1)}, bf16[128,1024]{1,0:T(8,128)(2,1)}, u32[]{:S(2)}, u32[]{:S(2)}) collective-permute-start(bf16[128,1024]{1,0:T(8,128)(2,1)} %keys_values.1.refs_0_), channel_id=1, source_target_pairs={{12,2},{13,3},{14,4},{15,5},{5,11},{28,18},{29,19},{30,20},{31,21}... | collective-permute-start | bytes 786440 | tf_op jit(solution)/shard_map/ppermute | solution.py:444
  98.9 20.2 %collective-permute-start.2 = (bf16[128,1024]{1,0:T(8,128)(2,1)}, bf16[128,1024]{1,0:T(8,128)(2,1)}, u32[]{:S(2)}, u32[]{:S(2)}) collective-permute-start(bf16[128,1024]{1,0:T(8,128)(2,1)} %keys_values.1.refs_0_), channel_id=1, source_target_pairs={{12,0},{13,1},{14,2},{15,3},{0,4},{1,5},{5,9},{6,10},{7,11},{28,16... | collective-permute-start | bytes 786440 | tf_op jit(solution)/shard_map/ppermute | solution.py:444
  101.0 20.9 %collective-permute-start.1 = (bf16[128,1024]{1,0:T(8,128)(2,1)}, bf16[128,1024]{1,0:T(8,128)(2,1)}, u32[]{:S(2)}, u32[]{:S(2)}) collective-permute-start(bf16[128,1024]{1,0:T(8,128)(2,1)} %keys_values.1.refs_0_), channel_id=1, source_target_pairs={{14,0},{15,1},{0,2},{1,3},{2,4},{3,5},{5,7},{6,8},{7,9},{8,10},{9,... | collective-permute-start | bytes 786440 | tf_op jit(solution)/shard_map/ppermute | solution.py:444
  104.3 0.9 copy-start.2
  105.1 31.6 %all-to-all-start.2 = ((bf16[32,16,768]{2,1,0:T(8,128)(2,1)}), bf16[32,16,768]{2,1,0:T(8,128)(2,1)S(1)}, u32[]{:S(2)}, u32[]{:S(2)}) async-start(bf16[32,16,768]{2,1,0:T(8,128)(2,1)} %copy-done.2), calls=%async_computation.2 | async-start | bytes 1572864 | tf_op jit(solution)/shard_map/all_to_all | solution.py:492
  111.7 15.9 %collective-permute-start.5 = (bf16[128,1024]{1,0:T(8,128)(2,1)}, bf16[128,1024]{1,0:T(8,128)(2,1)S(1)}, u32[]{:S(2)}, u32[]{:S(2)}) collective-permute-start(bf16[128,1024]{1,0:T(8,128)(2,1)} %keys_values.1.refs_0_), channel_id=1, source_target_pairs={{0,1},{2,3},{6,7},{8,9},{10,11},{12,13},{14,15},{16,17},{18,19},{2... | collective-permute-start | bytes 786440 | tf_op jit(solution)/shard_map/ppermute | solution.py:447
  113.8 1.2 copy-start.1
  115.1 1.0 copy-start.3
  121.9 5.7 %collective-permute-start.6 = (bf16[128,1024]{1,0:T(8,128)(2,1)}, bf16[128,1024]{1,0:T(8,128)(2,1)S(1)}, u32[]{:S(2)}, u32[]{:S(2)}) collective-permute-start(bf16[128,1024]{1,0:T(8,128)(2,1)} %collective-permute-done.1.refs_2_), channel_id=1, source_target_pairs={{0,1},{1,0},{2,3},{3,2},{5,4},{7,6},{8,9},{9,8},{10,11},{11,10},{1... | collective-permute-start | bytes 786440 | tf_op jit(solution)/shard_map/ppermute | solution.py:447
  123.8 3.8 %collective-permute-start.7 = (bf16[128,1024]{1,0:T(8,128)(2,1)}, bf16[128,1024]{1,0:T(8,128)(2,1)S(1)}, u32[]{:S(2)}, u32[]{:S(2)}) collective-permute-start(bf16[128,1024]{1,0:T(8,128)(2,1)} %collective-permute-done.2.refs_4_), channel_id=1, source_target_pairs={{0,1},{1,0},{2,3},{3,2},{5,4},{9,8},{10,11},{11,10},{16,17},{17,16... | collective-permute-start | bytes 786440 | tf_op jit(solution)/shard_map/ppermute | solution.py:447
  126.2 1.4 %collective-permute-start.8 = (bf16[128,1024]{1,0:T(8,128)(2,1)}, bf16[128,1024]{1,0:T(8,128)(2,1)S(1)}, u32[]{:S(2)}, u32[]{:S(2)}) collective-permute-start(bf16[128,1024]{1,0:T(8,128)(2,1)} %collective-permute-done.3.refs_6_), channel_id=1, source_target_pairs={{2,3},{3,2},{5,4},{11,10},{18,19},{19,18},{21,20},{27,26}} | collective-permute-start | bytes 786440 | tf_op jit(solution)/shard_map/ppermute | solution.py:447
  126.9 0.7 collective-permute-start.9
